TPU v7x, 32 devices: a whole 2x2x4 slice. The times are simulated.
32 devices in a mesh: col: 8 (over z, x), layer: 4 (over y, core).
Axes of the slice: x: 2, y: 2, z: 4, core: 2. Of those that a mesh axis runs over, the one named last changes fastest.
Arguments:
- tangents: bfloat16 [4, 128, 128, 512], P('layer', 'col'), may hold values from -120 to 120
- voltage: float32 [2, 4, 128, 128], P(None, 'layer', 'col'), may hold values from -0.2 to 0.6
- conductance: float32 [2, 4, 128, 128], P(None, 'layer', 'col'), may hold values from 0.5 to 5
- local_weights: bfloat16 [4, 128, 7, 128, 128], P('layer', 'col'), may hold values from 0 to 0.29882812
- block_label: int32 [4, 128], replicated, may hold values 0 or 1
- pair_dest: int32 [4, 8, 32, 1], P('layer', 'col'), may hold values from 0 to 7; in each aligned block of 32 rows (0 to 31, 32 to 63, ..., all dimensions but the last counted through in order) at most 8 rows name the same one
- pair_target: int32 [4, 8, 32], P('layer', 'col'), may hold values from 0 to 15
- bundle_source: int32 [4, 8, 8], P('layer', 'col'), may hold values from 0 to 15
- pair_weights: bfloat16 [4, 8, 32, 128, 128], P('layer', 'col'), may hold values from 0 to 0.29882812
Outputs:
- next_tangents: bfloat16 [4, 128, 128, 512], P('layer', 'col')
- growth: float32 [512], replicated
Inputs may be any that keep to these rules, and one draw needn't show every extreme that they name: `pair_dest`: within each group's 32 pairs no destination group is named more than 8 times, a bound that some block reaches.
All inputs are finite; a program needn't handle non-finite values.
Results may differ from a plain program's by a relative error of at most 0.019.
Values may be sent and summed in bfloat16 or wider, within the bound.
A program may use at most 192 MiB of HBM per device.

v0:
```python
import jax
import jax.numpy as jnp
from jax import lax
from jax.sharding import PartitionSpec as P

EXCITE_REVERSAL = 1.0
INHIBIT_REVERSAL = -0.5
THRESHOLD = 0.2
SIGMOID_WIDTH = 0.1
TIME_STEP = 0.1


def extended(cells, sides, width, closed):
    for axis, dim in sides:
        count = lax.axis_size(axis)
        ends = count if closed else count - 1
        head = lax.slice_in_dim(cells, 0, width, axis=dim)
        tail = lax.slice_in_dim(cells, cells.shape[dim] - width, cells.shape[dim], axis=dim)
        cells = jnp.concatenate(
            [
                lax.ppermute(tail, axis, [(i, (i + 1) % count) for i in range(ends)]),
                cells,
                lax.ppermute(head, axis, [((i + 1) % count, i) for i in range(ends)]),
            ],
            axis=dim,
        )
    return cells


def gain_slope(volt_now):
    sigma_value = jax.nn.sigmoid((volt_now - THRESHOLD) / SIGMOID_WIDTH)
    return sigma_value * (1.0 - sigma_value) / SIGMOID_WIDTH


def body(
    tangents,
    voltage,
    conductance,
    local_weights,
    block_label,
    pair_dest,
    pair_target,
    bundle_source,
    pair_weights,
):
    lay_blocks, col_blocks, block_size, vectors = tangents.shape
    blocks = lay_blocks * col_blocks
    col_count = lax.axis_size("col")
    lay_count = lax.axis_size("layer")
    destination = pair_dest[0, 0, :, 0]
    target_block = pair_target[0, 0]
    bundle_row = bundle_source[0, 0]
    pair_count = destination.shape[0]
    capacity = max(2, 2 * pair_count // col_count)
    slot_count = col_count * capacity
    lay_start = lax.axis_index("layer") * lay_blocks
    col_start = lax.axis_index("col") * col_blocks
    reversal = jnp.where(block_label == 1, INHIBIT_REVERSAL, EXCITE_REVERSAL).astype(jnp.float32)
    reversal_wide = jnp.concatenate([reversal[:, -2:], reversal, reversal[:, :2]], axis=1)
    reversal_columns = lax.dynamic_slice(
        reversal_wide, (lay_start, col_start), (lay_blocks, col_blocks + 4)
    )
    edge_row = jnp.full((1, reversal.shape[1]), EXCITE_REVERSAL, jnp.float32)
    reversal_tall = jnp.concatenate([edge_row, reversal, edge_row], axis=0)
    reversal_layers = lax.dynamic_slice(
        reversal_tall, (lay_start, col_start), (lay_blocks + 2, col_blocks)
    )
    pair_order = jnp.arange(pair_count, dtype=jnp.int32)
    earlier = (destination[:, None] == destination[None, :]) & (
        pair_order[None, :] < pair_order[:, None]
    )
    slot_rank = jnp.sum(earlier.astype(jnp.int32), axis=1)
    slot_index = destination * capacity + slot_rank
    placement = jnp.arange(slot_count, dtype=jnp.int32)[:, None] == slot_index[None, :]
    place_half = placement.astype(jnp.bfloat16)
    slot_target = (
        jnp.dot(placement.astype(jnp.float32), target_block.astype(jnp.float32))
        .astype(jnp.bfloat16)
        .reshape(col_count, capacity)
    )
    chosen = destination[:, None] == jnp.arange(col_count, dtype=jnp.int32)[None, :]
    source_block = jnp.sum(jnp.where(chosen, bundle_row[None, :], 0), axis=1)
    block_ids = jnp.arange(blocks, dtype=jnp.int32)
    own_pair_weights = pair_weights[0, 0]
    growth = jnp.zeros((vectors,), jnp.float32)
    for step_index in range(voltage.shape[0]):
        volt_now = voltage[step_index]
        conduct_now = conductance[step_index]
        scaled = (tangents * gain_slope(volt_now)[..., None]).astype(jnp.bfloat16)
        flat_scaled = scaled.reshape(blocks, block_size, vectors)
        sources = flat_scaled[source_block]
        products = jnp.einsum(
            "pij,pjk->pik", own_pair_weights, sources, preferred_element_type=jnp.float32
        ).astype(jnp.bfloat16)
        slot_data = jnp.dot(
            place_half, products.reshape(pair_count, -1), preferred_element_type=jnp.float32
        )
        slot_data = slot_data.astype(jnp.bfloat16).reshape(col_count, capacity, block_size, vectors)
        got_slots, arrival_target = (
            lax.all_to_all(slot_data, "col", split_axis=0, concat_axis=0, tiled=True),
            lax.all_to_all(slot_target, "col", split_axis=0, concat_axis=0, tiled=True),
        )
        received = got_slots.reshape(slot_count, -1)
        hit_table = (
            arrival_target.reshape(-1).astype(jnp.int32)[None, :] == block_ids[:, None]
        ).astype(jnp.bfloat16)
        distant = jnp.dot(hit_table, received, preferred_element_type=jnp.float32).reshape(
            lay_blocks, col_blocks, block_size, vectors
        )
        col_wide = extended(scaled, (("col", 1),), 2, True)
        lay_wide = extended(scaled, (("layer", 0),), 1, False)
        drive_sum = (EXCITE_REVERSAL - volt_now[..., None]) * distant
        for neighbour in range(7):
            if neighbour < 5:
                source_rows = col_wide[:, neighbour : neighbour + col_blocks]
                potential = reversal_columns[:, neighbour : neighbour + col_blocks]
            else:
                first_row = 2 * (neighbour - 5)
                source_rows = lay_wide[first_row : first_row + lay_blocks]
                potential = reversal_layers[first_row : first_row + lay_blocks]
            product_term = jnp.einsum(
                "lcij,lcjk->lcik",
                local_weights[:, :, neighbour],
                source_rows,
                preferred_element_type=jnp.float32,
            )
            drive_sum = (
                drive_sum + (potential[..., None, None] - volt_now[..., None]) * product_term
            )
        advanced = (tangents + TIME_STEP * (drive_sum - conduct_now[..., None] * tangents)).astype(
            jnp.bfloat16
        )
        flat_rows = advanced.reshape(-1, vectors)
        gram_part = lax.dot_general(
            flat_rows, flat_rows, (((0,), (0,)), ((), ())), preferred_element_type=jnp.float32
        )
        gram_total = lax.psum(gram_part, ("col", "layer"))
        gram_mean = gram_total / float(blocks * block_size * col_count * lay_count)
        lower_factor = jnp.linalg.cholesky(gram_mean)
        identity = jnp.eye(vectors, dtype=jnp.float32)
        lower_inverse = lax.linalg.triangular_solve(
            lower_factor, identity, left_side=True, lower=True
        )
        upper_inverse = lower_inverse.T.astype(jnp.bfloat16)
        growth = growth + jnp.log(jnp.diagonal(lower_factor))
        tangents = (
            jnp.dot(flat_rows, upper_inverse, preferred_element_type=jnp.float32)
            .astype(jnp.bfloat16)
            .reshape(advanced.shape)
        )
    return (tangents, growth)


def solution(mesh):
    in_specs = (
        P("layer", "col", None, None),
        P(None, "layer", "col", None),
        P(None, "layer", "col", None),
        P("layer", "col", None, None, None),
        P(),
        P("layer", "col", None, None),
        P("layer", "col", None),
        P("layer", "col", None),
        P("layer", "col", None, None, None),
    )
    out_specs = (P("layer", "col", None, None), P())
    return jax.shard_map(body, mesh=mesh, in_specs=in_specs, out_specs=out_specs, check_vma=False)
```

profile of v0, /device:TPU:25, one launch (start us, length us, event | category | flops | bytes accessed | tf_op | source)
XLA Modules:
  0.0 1191.2 jit_solution(7367253915485684778)
XLA Ops:
  32.6 8.0 copy.281
  40.6 7.7 convolution_convert_fusion.1
  85.1 88.1 %collective-permute-done = bf16[1,2,128,512]{3,1,2,0:T(2,128)(2,1)} collective-permute-done((bf16[1,2,128,512]{3,1,2,0:T(2,128)(2,1)}, bf16[1,2,128,512]{3,1,2,0:T(2,128)(2,1)}, u32[]{:S(2)}, u32[]{:S(2)}) %collective-permute-start) | collective-permute-done | bytes 262176 | tf_op jit(solution)/shard_map/ppermute | solution.py:21
  173.2 20.7 %collective-permute-done.1 = bf16[1,2,128,512]{3,1,2,0:T(2,128)(2,1)} collective-permute-done((bf16[1,2,128,512]{3,1,2,0:T(2,128)(2,1)}, bf16[1,2,128,512]{3,1,2,0:T(2,128)(2,1)}, u32[]{:S(2)}, u32[]{:S(2)}) %collective-permute-start.1) | collective-permute-done | bytes 262176 | tf_op jit(solution)/shard_map/ppermute | solution.py:23
  193.9 8.7 fusion.26
  220.9 14.0 %fusion.45 = f32[16,512,128]{1,2,0:T(8,128)} fusion(bf16[16,128,512]{2,0,1:T(8,128)(2,1)} %bitcast.35, bf16[1,16,7,128,128]{4,3,2,1,0:T(8,128)(2,1)S(1)} %copy-done.6), kind=kOutput, calls=%fused_computation.100 | convolution fusion | flops 268435456 | bytes 6815744 | tf_op jit(solution)/shard_map/lcij,lcjk->lcik/dot_general | solution.py:121
  242.4 32.5 %fusion.9 = bf16[1,16,128,512]{3,1,2,0:T(8,128)(2,1)} fusion(f32[16,512,128]{1,2,0:T(8,128)} %fusion.43, f32[16,512,128]{1,2,0:T(8,128)} %fusion.45, f32[16,512,128]{1,2,0:T(8,128)} %fusion.47, f32[16,512,128]{1,2,0:T(8,128)} %fusion.49, f32[16,512,128]{1,2,0:T(8,128)} %fusion.95, f32[16,512,128]{1,2,0:T(8,128)} %fusion.51, f32[16,512,128]{1,2,0:T(8,128)} %fusion.53, ...), kind=kOutput, calls=%fused_computation.22 | convolution fusion | flops 156238848 | bytes 42017024 | tf_op jit(solution)/shard_map/dot_general | solution.py:107
  283.3 169.5 %all-reduce.4.cloned.1.call-done = f32[512,512]{0,1:T(8,128)} async-done(((f32[512,512]{0,1:T(8,128)}), f32[512,512]{0,1:T(8,128)}) %all-reduce.4.cloned.1.call-update) | async-done | bytes 1048592 | tf_op jit(solution)/shard_map/psum | solution.py:137
  460.4 11.7 cholesky.286
  472.8 9.8 custom-call.31
  486.9 12.2 %cholesky.305 = f32[128,128]{1,0:T(8,128)S(1)} custom-call(f32[128,128]{1,0:T(8,128)S(1)} %cholesky.430), custom_call_target="Cholesky" | custom-call | tf_op jit(solution)/shard_map/jit(cholesky)/cholesky | solution.py:139
  500.5 9.8 custom-call.32
  512.6 11.7 cholesky.326
  525.7 9.8 custom-call.33
  537.7 11.9 cholesky.343
  556.2 11.6 while.4
  568.6 40.1 %custom-call.34 = f32[4,128,128]{1,2,0:T(8,128)S(1)} custom-call(f32[4,128,128]{2,1,0:T(8,128)} %copy-done.15), custom_call_target="InvertDiagBlocksLowerTriangular" | custom-call | tf_op jit(solution)/shard_map/triangular_solve/custom-call.3 | solution.py:141
  627.9 7.9 copy.282
  635.7 7.7 convolution_convert_fusion
  668.0 121.7 %collective-permute-done.5 = bf16[1,2,128,512]{3,2,1,0:T(8,128)(2,1)S(1)} collective-permute-done((bf16[1,2,128,512]{3,2,1,0:T(8,128)(2,1)S(1)}, bf16[1,2,128,512]{3,2,1,0:T(8,128)(2,1)S(1)}, u32[]{:S(2)}, u32[]{:S(2)}) %collective-permute-start.5) | collective-permute-done | bytes 262176 | tf_op jit(solution)/shard_map/ppermute | solution.py:23
  807.2 31.2 %all-to-all-done.2 = bf16[8,8,128,512]{3,1,2,0:T(8,128)(2,1)} async-done(((bf16[8,8,128,512]{3,1,2,0:T(8,128)(2,1)}), bf16[8,8,128,512]{3,1,2,0:T(8,128)(2,1)}, u32[]{:S(2)}, u32[]{:S(2)}) %all-to-all-start.2) | async-done | bytes 8388640 | tf_op jit(solution)/shard_map/all_to_all | solution.py:100
  838.4 37.8 %fusion.13 = bf16[16,128,512]{2,0,1:T(8,128)(2,1)} fusion(f32[16,512,128]{1,2,0:T(8,128)} %fusion.37, f32[16,512,128]{1,2,0:T(8,128)} %fusion.39, f32[16,512,128]{1,2,0:T(8,128)} %fusion.28, f32[16,512,128]{1,2,0:T(8,128)} %fusion.17, f32[16,512,128]{1,2,0:T(8,128)} %fusion.97, f32[16,512,128]{1,2,0:T(8,128)} %fusion.32, f32[16,512,128]{1,2,0:T(8,128)} %fusion.21, ...), kind=kOutput, calls=%fused_computation.27 | convolution fusion | flops 155190272 | bytes 44114176 | tf_op jit(solution)/shard_map/dot_general | solution.py:107
  889.5 134.8 %all-reduce.6.cloned.1.call-done = f32[512,512]{0,1:T(8,128)} async-done(((f32[512,512]{0,1:T(8,128)}), f32[512,512]{0,1:T(8,128)}) %all-reduce.6.cloned.1.call-update) | async-done | bytes 1048592 | tf_op jit(solution)/shard_map/psum | solution.py:137
  1029.5 11.7 cholesky.358
  1041.8 9.8 custom-call.35
  1054.3 11.9 cholesky.377
  1066.9 9.8 custom-call.36
  1078.4 11.7 cholesky.398
  1090.8 9.8 custom-call.37
  1102.0 12.0 %cholesky.415 = f32[128,128]{1,0:T(8,128)S(1)} custom-call(f32[128,128]{1,0:T(8,128)S(1)} %convolution_subtract_fusion.10), custom_call_target="Cholesky" | custom-call | tf_op jit(solution)/shard_map/jit(cholesky)/cholesky | solution.py:139
  1124.2 11.2 while.5
  1135.3 39.3 %custom-call.38 = f32[4,128,128]{1,2,0:T(8,128)S(1)} custom-call(f32[4,128,128]{2,1,0:T(8,128)S(1)} %get-tuple-element.19), custom_call_target="InvertDiagBlocksLowerTriangular" | custom-call | tf_op jit(solution)/shard_map/triangular_solve/custom-call.3 | solution.py:141
  (243 shorter events, 247.9 us)
Async XLA Ops:
  7.2 20.0 %copy-start = (bf16[1,1,32,128,128]{4,3,2,1,0:T(8,128)(2,1)S(1)}, bf16[1,1,32,128,128]{4,3,2,1,0:T(8,128)(2,1)}, u32[]{:S(2)}) copy-start(bf16[1,1,32,128,128]{4,3,2,1,0:T(8,128)(2,1)} %param.20) | copy-start | bytes 3145732
  8.8 31.8 %copy-start.29 = (s32[32]{0:T(128)}, s32[32]{0:T(128)S(1)}, u32[]{:S(2)}) copy-start(s32[32]{0:T(128)S(1)} %multiply_add_fusion) | copy-start | bytes 388
  10.3 38.0 %all-to-all-start = ((bf16[8,1,8]{2,1,0:T(2,128)(2,1)}), bf16[8,1,8]{2,1,0:T(2,128)(2,1)S(1)}, u32[]{:S(2)}, u32[]{:S(2)}) async-start(bf16[8,1,8]{2,1,0:T(2,128)(2,1)} %all_to_all.17), calls=%async_computation | async-start | bytes 8192 | tf_op jit(solution)/shard_map/all_to_all | solution.py:101
  17.2 7.2 copy-start.27
  48.9 193.5 %all-to-all-start.1 = ((bf16[8,8,128,512]{3,1,2,0:T(8,128)(2,1)}), bf16[8,8,128,512]{3,1,2,0:T(8,128)(2,1)}, u32[]{:S(2)}, u32[]{:S(2)}) async-start(bf16[8,8,128,512]{3,1,2,0:T(8,128)(2,1)} %bitcast.391), calls=%async_computation.1 | async-start | bytes 16777216 | tf_op jit(solution)/shard_map/all_to_all | solution.py:100
  54.5 14.8 %copy-start.16 = (f32[2,1,16,128]{3,2,1,0:T(8,128)S(1)}, f32[2,1,16,128]{3,2,1,0:T(8,128)}, u32[]{:S(2)}) copy-start(f32[2,1,16,128]{3,2,1,0:T(8,128)} %param.13) | copy-start | bytes 49156
  54.5 398.4 %all-reduce.4.cloned.1.call-start = ((), (), s32[]{:S(2)}) async-start(), calls=%async_computation.3 | async-start | bytes 2097152 | tf_op jit(solution)/shard_map/psum | solution.py:137
  57.0 19.4 %copy-start.25 = (f32[2,1,16,128]{3,2,1,0:T(8,128)S(1)}, f32[2,1,16,128]{3,2,1,0:T(8,128)}, u32[]{:S(2)}) copy-start(f32[2,1,16,128]{3,2,1,0:T(8,128)} %param.14) | copy-start | bytes 49156
  57.0 163.9 %collective-permute-start.2 = (bf16[1,16,128,512]{3,1,2,0:T(8,128)(2,1)}, bf16[1,16,128,512]{3,1,2,0:T(8,128)(2,1)}, u32[]{:S(2)}, u32[]{:S(2)}) collective-permute-start(bf16[1,16,128,512]{3,1,2,0:T(8,128)(2,1)} %fusion.6), channel_id=1, source_target_pairs={{0,1},{1,2},{2,3},{4,5},{5,6},{6,7},{8,9},{9,10},{10,11},{12,13},{... | collective-permute-start | bytes 6291464 | tf_op jit(solution)/shard_map/ppermute | solution.py:21
  62.0 172.9 %collective-permute-start.3 = (bf16[1,16,128,512]{3,1,2,0:T(8,128)(2,1)}, bf16[1,16,128,512]{3,1,2,0:T(8,128)(2,1)}, u32[]{:S(2)}, u32[]{:S(2)}) collective-permute-start(bf16[1,16,128,512]{3,1,2,0:T(8,128)(2,1)} %fusion.6), channel_id=1, source_target_pairs={{1,0},{2,1},{3,2},{5,4},{6,5},{7,6},{9,8},{10,9},{11,10},{13,12},{... | collective-permute-start | bytes 6291464 | tf_op jit(solution)/shard_map/ppermute | solution.py:23
  66.7 106.5 %collective-permute-start = (bf16[1,2,128,512]{3,1,2,0:T(2,128)(2,1)}, bf16[1,2,128,512]{3,1,2,0:T(2,128)(2,1)}, u32[]{:S(2)}, u32[]{:S(2)}) collective-permute-start(bf16[1,2,128,512]{3,1,2,0:T(2,128)(2,1)} %get-tuple-element.52), channel_id=1, source_target_pairs={{0,4},{4,8},{8,12},{12,16},{16,20},{20,24},{24,28},{28,0},{1,5},{5... | collective-permute-start | bytes 786440 | tf_op jit(solution)/shard_map/ppermute | solution.py:21
  67.9 126.0 %collective-permute-start.1 = (bf16[1,2,128,512]{3,1,2,0:T(2,128)(2,1)}, bf16[1,2,128,512]{3,1,2,0:T(2,128)(2,1)}, u32[]{:S(2)}, u32[]{:S(2)}) collective-permute-start(bf16[1,2,128,512]{3,1,2,0:T(2,128)(2,1)} %get-tuple-element.53), channel_id=1, source_target_pairs={{4,0},{8,4},{12,8},{16,12},{20,16},{24,20},{28,24},{0,28},{5,1},{9... | collective-permute-start | bytes 786440 | tf_op jit(solution)/shard_map/ppermute | solution.py:23
  85.1 117.5 %copy-start.6 = (bf16[1,16,7,128,128]{4,3,2,1,0:T(8,128)(2,1)S(1)}, bf16[1,16,7,128,128]{4,3,2,1,0:T(8,128)(2,1)}, u32[]{:S(2)}) copy-start(bf16[1,16,7,128,128]{4,3,2,1,0:T(8,128)(2,1)} %param.15) | copy-start | bytes 11010052
  627.9 7.9 copy-start.30
  643.4 195.0 %all-to-all-start.2 = ((bf16[8,8,128,512]{3,1,2,0:T(8,128)(2,1)}), bf16[8,8,128,512]{3,1,2,0:T(8,128)(2,1)}, u32[]{:S(2)}, u32[]{:S(2)}) async-start(bf16[8,8,128,512]{3,1,2,0:T(8,128)(2,1)} %bitcast.392), calls=%async_computation.2 | async-start | bytes 16777216 | tf_op jit(solution)/shard_map/all_to_all | solution.py:100
  650.4 6.4 copy-start.23
  650.4 6.5 copy-start.24
  650.4 6.6 copy-start.22
  650.4 6.7 copy-start.21
  650.4 6.8 copy-start.20
  650.5 6.9 copy-start.19
  650.5 7.0 copy-start.18
  650.5 7.1 copy-start.17
  650.5 373.8 %all-reduce.6.cloned.1.call-start = ((), (), s32[]{:S(2)}) async-start(), calls=%async_computation.4 | async-start | bytes 2097152 | tf_op jit(solution)/shard_map/psum | solution.py:137
  653.1 147.2 %collective-permute-start.7 = (bf16[1,16,128,512]{3,2,1,0:T(8,128)(2,1)S(1)}, bf16[1,16,128,512]{3,2,1,0:T(8,128)(2,1)}, u32[]{:S(2)}, u32[]{:S(2)}) collective-permute-start(bf16[1,16,128,512]{3,2,1,0:T(8,128)(2,1)S(1)} %multiply_convert_fusion), channel_id=1, source_target_pairs={{1,0},{2,1},{3,2},{5,4},{6,5},{7,6},{9,8},{10,9},{11,10},{13,12},{... | collective-permute-start | bytes 6291464 | tf_op jit(solution)/shard_map/ppermute | solution.py:23
  657.8 132.0 %copy-start.7 = (bf16[1,16,7,128,128]{4,3,2,1,0:T(8,128)(2,1)S(1)}, bf16[1,16,7,128,128]{4,3,2,1,0:T(8,128)(2,1)}, u32[]{:S(2)}) copy-start(bf16[1,16,7,128,128]{4,3,2,1,0:T(8,128)(2,1)} %param.15) | copy-start | bytes 11010052
  657.8 146.8 %collective-permute-start.6 = (bf16[1,16,128,512]{3,2,1,0:T(8,128)(2,1)S(1)}, bf16[1,16,128,512]{3,2,1,0:T(8,128)(2,1)S(1)}, u32[]{:S(2)}, u32[]{:S(2)}) collective-permute-start(bf16[1,16,128,512]{3,2,1,0:T(8,128)(2,1)S(1)} %multiply_convert_fusion), channel_id=1, source_target_pairs={{0,1},{1,2},{2,3},{4,5},{5,6},{6,7},{8,9},{9,10},{10,11},{12,13},{... | collective-permute-start | bytes 6291464 | tf_op jit(solution)/shard_map/ppermute | solution.py:21
  661.1 133.9 %collective-permute-start.4 = (bf16[1,2,128,512]{3,2,1,0:T(8,128)(2,1)S(1)}, bf16[1,2,128,512]{3,2,1,0:T(8,128)(2,1)S(1)}, u32[]{:S(2)}, u32[]{:S(2)}) collective-permute-start(bf16[1,2,128,512]{3,2,1,0:T(8,128)(2,1)S(1)} %get-tuple-element.48), channel_id=1, source_target_pairs={{0,4},{4,8},{8,12},{12,16},{16,20},{20,24},{24,28},{28,0},{1,5},{5... | collective-permute-start | bytes 786440 | tf_op jit(solution)/shard_map/ppermute | solution.py:21
  662.3 127.4 %collective-permute-start.5 = (bf16[1,2,128,512]{3,2,1,0:T(8,128)(2,1)S(1)}, bf16[1,2,128,512]{3,2,1,0:T(8,128)(2,1)S(1)}, u32[]{:S(2)}, u32[]{:S(2)}) collective-permute-start(bf16[1,2,128,512]{3,2,1,0:T(8,128)(2,1)S(1)} %get-tuple-element.49), channel_id=1, source_target_pairs={{4,0},{8,4},{12,8},{16,12},{20,16},{24,20},{28,24},{0,28},{5,1},{9... | collective-permute-start | bytes 786440 | tf_op jit(solution)/shard_map/ppermute | solution.py:23
  804.5 33.9 %copy-start.28 = (s32[64]{0:T(128)S(1)}, s32[64]{0:T(128)}, u32[]{:S(2)}) copy-start(s32[64]{0:T(128)} %reshape.769) | copy-start | bytes 772
  1077.0 97.7 %copy-start.8 = (f32[512,512]{1,0:T(8,128)S(1)}, f32[512,512]{1,0:T(8,128)}, u32[]{:S(2)}) copy-start(f32[512,512]{1,0:T(8,128)} %fusion.70) | copy-start | bytes 3145732
  1174.7 6.6 copy-start.14
  (12 other events, 29.9 us)
Sparse Core Ops, SparseCore 0:
  279.6 173.1 all-reduce.3
  881.0 143.2 all-reduce.5
where the time goes:
time: 1210 us; the launch traced here: 1190 us
  waiting for transfers between devices  567 us (47%)
  other arithmetic  278 us (23%)
  matrix products  204 us (17%)
  local copies, waits for them, and re-layouts  85.4 us (7%)
  starting transfers between devices  36.9 us (3%)
  between operations  20 us (2%)
    psum x2, waiting for transfers between devices, body(): gram_total = lax.psum(gram_part, ('col', 'layer'))  304 us
    another operation x30, other arithmetic, body(): lower_factor = jnp.linalg.cholesky(gram_mean)  161 us
    ppermute x4, waiting for transfers between devices, extended(): lax.ppermute(head, axis, [((i + 1) % count, i) for i in range(ends)])  142 us
    ppermute x4, waiting for transfers between devices, extended(): lax.ppermute(tail, axis, [(i, (i + 1) % count) for i in range(ends)])  88.2 us
    another operation x5, other arithmetic, body(): lax.linalg.triangular_solve(lower_factor, identity, left_side=True, lower...  84.7 us
    dot_general x2, matrix products, body(): jnp.dot(hit_table, received, preferred_element_type=jnp.float32)  70.3 us
    dot_general x14, matrix products, body(): jnp.einsum('lcij,lcjk->lcik', local_weights[:, :, neighbour], source_rows...  66.8 us
    all_to_all x2, waiting for transfers between devices, body(): lax.all_to_all(slot_data, 'col', split_axis=0, concat_axis=0, tiled=True)  32.6 us
  transfers between devices with their start and end apart: 13, of which 7 were waited for; matrix products, arithmetic and copies ran while one was open for 12% of the time, Pallas kernels for 0%

commit v1 on v0

v1 whole, which is shorter than its diff:
```python
import functools

import jax
import jax.numpy as jnp
from jax import lax
from jax.experimental import pallas as pl
from jax.experimental.pallas import tpu as pltpu
from jax.sharding import PartitionSpec as P

EXCITE_REVERSAL = 1.0
INHIBIT_REVERSAL = -0.5
THRESHOLD = 0.2
SIGMOID_WIDTH = 0.1
TIME_STEP = 0.1
HI = lax.Precision.HIGHEST
NB = 128
ROWS = 8


def inverse_factor(block):
    n = block.shape[0]
    lane = lax.broadcasted_iota(jnp.int32, (ROWS, n), 1)
    sub = lax.broadcasted_iota(jnp.int32, (ROWS, n), 0)
    tiles = [block[t * ROWS : (t + 1) * ROWS] for t in range(n // ROWS)]
    for first in range(n // ROWS):
        start = first * ROWS
        inside = (lane >= start) & (lane < start + ROWS)
        head = tiles[first]
        cols = [jnp.broadcast_to(head[:, start + q : start + q + 1], (ROWS, n)) for q in range(ROWS)]
        head = jnp.where(lane == sub + start, 1.0, jnp.where(inside, 0.0, head))
        pivots, crossed, kept = [], [], []
        scale = jnp.zeros((ROWS, n), jnp.float32)
        for q in range(ROWS):
            pivot = cols[q][q : q + 1]
            inv = 1.0 / pivot
            factor = jnp.where(sub > q, cols[q] * inv, 0.0)
            ahead = {r: cols[r][q : q + 1] for r in range(q + 1, ROWS)}
            for r in range(q + 1, ROWS):
                cols[r] = cols[r] - factor * ahead[r]
            row = head[q : q + 1]
            head = head - factor * row
            scale = jnp.where(sub == q, lax.rsqrt(pivot), scale)
            pivots.append(inv)
            crossed.append(ahead)
            kept.append(row)
        tiles[first] = head * scale
        for t in range(first + 1, n // ROWS):
            tile = tiles[t]
            cols_t = [jnp.broadcast_to(tile[:, start + q : start + q + 1], (ROWS, n)) for q in range(ROWS)]
            tile = jnp.where(inside, 0.0, tile)
            for q in range(ROWS):
                factor = cols_t[q] * pivots[q]
                for r in range(q + 1, ROWS):
                    cols_t[r] = cols_t[r] - factor * crossed[q][r]
                tile = tile - factor * kept[q]
            tiles[t] = tile
    out = jnp.concatenate(tiles, axis=0)
    rows_id = lax.broadcasted_iota(jnp.int32, (n, n), 0)
    cols_id = lax.broadcasted_iota(jnp.int32, (n, n), 1)
    return jnp.where(rows_id >= cols_id, out, 0.0)


def orthonormal_kernel(count, gram_ref, upper_ref, growth_ref, work):
    n = gram_ref.shape[0]
    work[...] = gram_ref[...] * (1.0 / count)
    cols_id = lax.broadcasted_iota(jnp.int32, (NB, n), 1)

    def step(i, carry):
        at = pl.multiple_of(i * NB, NB)
        diag = inverse_factor(work[pl.ds(at, NB), pl.ds(at, NB)])
        work[:, pl.ds(at, NB)] = jnp.zeros((n, NB), jnp.float32)
        rows = jnp.dot(diag, work[pl.ds(at, NB), :], precision=HI, preferred_element_type=jnp.float32)
        work[pl.ds(at, NB), :] = rows
        work[pl.ds(at, NB), pl.ds(at, NB)] = diag
        rows = work[pl.ds(at, NB), :]
        panel = jnp.where(cols_id >= at + NB, rows, 0.0)
        work[...] -= lax.dot_general(
            panel, rows, (((0,), (0,)), ((), ())), precision=HI, preferred_element_type=jnp.float32
        )
        return carry

    lax.fori_loop(0, n // NB, step, 0)
    rows_n = lax.broadcasted_iota(jnp.int32, (n, n), 0)
    cols_n = lax.broadcasted_iota(jnp.int32, (n, n), 1)
    full = work[...]
    upper_ref[...] = jnp.where(rows_n >= cols_n, full, 0.0).T.astype(jnp.bfloat16)
    growth_ref[...] = -jnp.log(jnp.sum(jnp.where(rows_n == cols_n, full, 0.0), axis=0, keepdims=True))


def orthonormalize(gram_total, count):
    n = gram_total.shape[0]
    upper, growth = pl.pallas_call(
        functools.partial(orthonormal_kernel, count),
        out_shape=(
            jax.ShapeDtypeStruct((n, n), jnp.bfloat16),
            jax.ShapeDtypeStruct((1, n), jnp.float32),
        ),
        in_specs=[pl.BlockSpec(memory_space=pltpu.VMEM)],
        out_specs=(pl.BlockSpec(memory_space=pltpu.VMEM), pl.BlockSpec(memory_space=pltpu.VMEM)),
        scratch_shapes=[pltpu.VMEM((n, n), jnp.float32)],
        compiler_params=pltpu.CompilerParams(vmem_limit_bytes=32 * 1024 * 1024),
        name="orthonormalize",
    )(gram_total)
    return upper, growth[0]


def gain_slope(volt_now):
    sigma_value = jax.nn.sigmoid((volt_now - THRESHOLD) / SIGMOID_WIDTH)
    return sigma_value * (1.0 - sigma_value) / SIGMOID_WIDTH


def shifted(value, axis, step, closed):
    count = lax.axis_size(axis)
    pairs = [(i, i + step) for i in range(count)]
    if closed:
        pairs = [(i, j % count) for i, j in pairs]
    else:
        pairs = [(i, j) for i, j in pairs if 0 <= j < count]
    return lax.ppermute(value, axis, pairs)


def neighbours(cells):
    before = shifted(cells[-2:], "col", 1, True)
    after = shifted(cells[:2], "col", -1, True)
    above = shifted(cells, "layer", 1, False)
    below = shifted(cells, "layer", -1, False)
    return before, after, above, below


def exchanged(value):
    return lax.all_to_all(value, "col", split_axis=0, concat_axis=0, tiled=True)


def advance_kernel(
    per_step, tangents_ref, before_ref, own_ref, after_ref, above_ref, below_ref, far_ref,
    weights_ref, far_weights_ref, coef_ref, advanced_ref, gram_ref, wide
):
    index = pl.program_id(0)
    blocks, size, _ = own_ref.shape

    @pl.when(index == 0)
    def _():
        wide[0:2] = before_ref[...]
        wide[2 : 2 + blocks] = own_ref[...]
        wide[2 + blocks : 4 + blocks] = after_ref[...]
        gram_ref[...] = jnp.zeros_like(gram_ref)

    for k in range(per_step):
        at = index * per_step + k
        coef = coef_ref[k]

        def times(weight, source):
            return jnp.dot(weight, source, preferred_element_type=jnp.float32)

        drive = coef[:, 7:8] * times(far_weights_ref[k], far_ref[...])
        for j in range(5):
            drive += coef[:, j : j + 1] * times(weights_ref[k, j], wide[at + j])
        drive += coef[:, 5:6] * times(weights_ref[k, 5], above_ref[at])
        drive += coef[:, 6:7] * times(weights_ref[k, 6], below_ref[at])
        now = tangents_ref[k].astype(jnp.float32)
        advanced_ref[k] = (now + TIME_STEP * (drive - coef[:, 8:9] * now)).astype(jnp.bfloat16)
    rows = advanced_ref[...].reshape(per_step * size, advanced_ref.shape[-1])
    gram_ref[...] += lax.dot_general(
        rows, rows, (((0,), (0,)), ((), ())), preferred_element_type=jnp.float32
    )


def advance(tangents, before, own, after, above, below, far, weights, far_weights, coef):
    blocks, size, vectors = tangents.shape
    per_step = 2 if blocks % 2 == 0 else 1
    whole = pl.BlockSpec(memory_space=pltpu.VMEM)

    def split(*rest):
        return pl.BlockSpec((per_step,) + rest, lambda i: (i,) + (0,) * len(rest))

    return pl.pallas_call(
        functools.partial(advance_kernel, per_step),
        grid=(blocks // per_step,),
        out_shape=(
            jax.ShapeDtypeStruct(tangents.shape, jnp.bfloat16),
            jax.ShapeDtypeStruct((vectors, vectors), jnp.float32),
        ),
        in_specs=[
            split(size, vectors),
            whole, whole, whole, whole, whole, whole,
            split(7, size, size),
            split(size, far.shape[0]),
            split(size, coef.shape[-1]),
        ],
        out_specs=(split(size, vectors), pl.BlockSpec((vectors, vectors), lambda i: (0, 0))),
        scratch_shapes=[pltpu.VMEM((blocks + 4, size, vectors), jnp.bfloat16)],
        compiler_params=pltpu.CompilerParams(
            vmem_limit_bytes=48 * 1024 * 1024, dimension_semantics=("arbitrary",)
        ),
        name="advance",
    )(tangents, before, own, after, above, below, far, weights, far_weights, coef)


def body(
    tangents,
    voltage,
    conductance,
    local_weights,
    block_label,
    pair_dest,
    pair_target,
    bundle_source,
    pair_weights,
):
    lay_blocks, col_blocks, size, vectors = tangents.shape
    steps = voltage.shape[0]
    blocks = col_blocks
    col_count = lax.axis_size("col")
    lay_count = lax.axis_size("layer")
    destination = pair_dest[0, 0, :, 0]
    target_block = pair_target[0, 0]
    bundle_row = bundle_source[0, 0]
    pair_count = destination.shape[0]
    capacity = max(2, 2 * pair_count // col_count)
    slot_count = col_count * capacity
    neurons = float(blocks * size * col_count * lay_count)
    layer = lax.axis_index("layer")
    col_start = lax.axis_index("col") * blocks

    pair_order = jnp.arange(pair_count, dtype=jnp.int32)
    earlier = (destination[:, None] == destination[None, :]) & (
        pair_order[None, :] < pair_order[:, None]
    )
    slot_index = destination * capacity + jnp.sum(earlier.astype(jnp.int32), axis=1)
    placement = jnp.arange(slot_count, dtype=jnp.int32)[:, None] == slot_index[None, :]
    slot_target = jnp.sum(jnp.where(placement, target_block[None, :], 0), axis=1)
    slot_weights = jnp.dot(
        placement.astype(jnp.bfloat16),
        pair_weights[0, 0].reshape(pair_count, size * size),
        preferred_element_type=jnp.float32,
    ).astype(jnp.bfloat16)
    bundle_pick = (
        bundle_row[:, None] == jnp.arange(blocks, dtype=jnp.int32)[None, :]
    )

    def bundle(cells):
        picked = jnp.dot(
            bundle_pick.astype(jnp.bfloat16), cells.reshape(blocks, -1),
            preferred_element_type=jnp.float32,
        )
        return picked.astype(jnp.bfloat16).reshape(col_count, size, vectors)

    volt = voltage[:, 0]
    slope = gain_slope(volt)
    state = tangents[0]
    scaled = (state * slope[0][..., None]).astype(jnp.bfloat16)
    edges = neighbours(scaled)
    far = exchanged(bundle(scaled))
    got_weights = exchanged(slot_weights.reshape(col_count, capacity, size * size))
    got_target = exchanged(slot_target.astype(jnp.int32).reshape(col_count, 1, capacity))
    bundle_slope = jnp.sum(jnp.where(bundle_pick[:, :, None, None], slope.transpose(1, 0, 2)[None], 0.0), axis=1)
    far_slope = exchanged(bundle_slope)
    edge_slope = [
        edge.transpose(1, 0, 2) for edge in neighbours(slope.transpose(1, 0, 2))
    ]
    hit = (
        got_target.reshape(col_count, 1, capacity)
        == jnp.arange(blocks, dtype=jnp.int32)[None, :, None]
    ).astype(jnp.bfloat16)
    far_weights = (
        lax.dot_general(
            hit, got_weights, (((2,), (1,)), ((0,), (0,))), preferred_element_type=jnp.float32
        )
        .astype(jnp.bfloat16)
        .reshape(col_count, blocks, size, size)
        .transpose(1, 2, 0, 3)
        .reshape(blocks, size, col_count * size)
    )

    reversal = jnp.where(block_label == 1, INHIBIT_REVERSAL, EXCITE_REVERSAL).astype(jnp.float32)
    edge_row = jnp.full((1, reversal.shape[1]), EXCITE_REVERSAL, jnp.float32)
    reversal = jnp.concatenate([edge_row, reversal, edge_row], axis=0)
    reversal = jnp.concatenate([reversal[:, -2:], reversal, reversal[:, :2]], axis=1)
    near = lax.dynamic_slice(reversal, (layer, col_start), (3, blocks + 4))
    potential = jnp.stack(
        [near[1, j : j + blocks] for j in range(5)]
        + [near[0, 2 : 2 + blocks], near[2, 2 : 2 + blocks], jnp.full((blocks,), EXCITE_REVERSAL)],
        axis=-1,
    )

    growth = jnp.zeros((vectors,), jnp.float32)
    for t in range(steps):
        coef = jnp.concatenate(
            [
                potential[:, None, :] - volt[t][..., None],
                conductance[t, 0][..., None],
                jnp.zeros((blocks, size, 7), jnp.float32),
            ],
            axis=-1,
        )
        advanced, gram = advance(
            state, edges[0], scaled, edges[1], edges[2], edges[3],
            far.reshape(col_count * size, vectors), local_weights[0], far_weights, coef,
        )
        gram = lax.psum(gram, ("col", "layer"))
        last = t == steps - 1
        if not last:
            edges = neighbours(advanced)
            far = exchanged(bundle(advanced))
        upper, grown = orthonormalize(gram, neurons)
        growth = growth + grown

        def rotated(cells):
            return jnp.dot(cells, upper, preferred_element_type=jnp.float32).astype(jnp.bfloat16)

        state = rotated(advanced)
        if not last:
            scaled = (state * slope[t + 1][..., None]).astype(jnp.bfloat16)
            edges = [
                (rotated(edge) * edge_slope[k][t + 1][..., None]).astype(jnp.bfloat16)
                for k, edge in enumerate(edges)
            ]
            far = (rotated(far) * far_slope[:, t + 1, :, None]).astype(jnp.bfloat16)
    return state[None], growth


def solution(mesh):
    in_specs = (
        P("layer", "col", None, None),
        P(None, "layer", "col", None),
        P(None, "layer", "col", None),
        P("layer", "col", None, None, None),
        P(),
        P("layer", "col", None, None),
        P("layer", "col", None),
        P("layer", "col", None),
        P("layer", "col", None, None, None),
    )
    out_specs = (P("layer", "col", None, None), P())
    return jax.shard_map(body, mesh=mesh, in_specs=in_specs, out_specs=out_specs, check_vma=False)
```

time: 1210 us -> 512 us (0.42); the launches traced: 1190 us -> 506 us
  waiting for transfers between devices: 567 us -> 296 us
  other arithmetic: 278 us -> 7.76 us
  matrix products: 204 us -> 25.4 us
  Pallas kernels: 0 us -> 74.5 us
  local copies, waits for them, and re-layouts: 85.4 us -> 33.9 us
  starting transfers between devices: 36.9 us -> 54 us
    another operation x36 -> x0, other arithmetic: 254 us -> none  [the longest x30 161 us: body(): lower_factor = jnp.linalg.cholesky(gram_mean)]
    ppermute x8 -> x12, waiting for transfers between devices: 231 us -> 0.03 us  [shifted(): return lax.ppermute(value, axis, pairs)]
    dot_general x25 -> x11, matrix products: 177 us -> 25.4 us  [the longest x7 17.9 us: rotated(): jnp.dot(cells, upper, preferred_element_type=jnp.float32)]
    pallas_call x0 -> x4, Pallas kernels: none -> 74.5 us  [the longest x2 43.8 us: orthonormalize(): pl.pallas_call(functools.partial(orthonormal_kernel, count), out_shape=(j...]
    psum x2, waiting for transfers between devices: 304 us -> 265 us  [body(): gram = lax.psum(gram, ('col', 'layer'))]
    another operation x26 -> x0, matrix products: 26.4 us -> none  [the longest x12 13.3 us: body(): lower_factor = jnp.linalg.cholesky(gram_mean)]
    another operation x35 -> x8, local copies, waits for them, and re-layouts: 24 us -> 2.9 us  [the longest x3 2.73 us: body(): conductance[t, 0][..., None]]
    reshape x1 -> x5, local copies, waits for them, and re-layouts: 1.17 us -> 16.2 us  [the longest x2 12.9 us: body(): far_weights = lax.dot_general(hit, got_weights, (((2,), (1,)), ((0,), (0,...]
  transfers between devices with their start and end apart: 13 -> 19, of which waited for: 7 -> 3; matrix products, arithmetic and copies ran while one was open for 12% -> 10% of each run, Pallas kernels for 0% -> 7%
where the time goes in v1:
time: 512 us; the launch traced here: 506 us
  waiting for transfers between devices  296 us (58%)
  Pallas kernels  74.5 us (15%)
  starting transfers between devices  54 us (11%)
  local copies, waits for them, and re-layouts  33.9 us (7%)
  matrix products  25.4 us (5%)
  between operations  14.4 us (3%)
  other arithmetic  7.76 us (2%)
    psum x2, waiting for transfers between devices, body(): gram = lax.psum(gram, ('col', 'layer'))  265 us
    pallas_call x2, Pallas kernels, orthonormalize(): pl.pallas_call(functools.partial(orthonormal_kernel, count), out_shape=(j...  43.8 us
    all_to_all x5, waiting for transfers between devices, exchanged(): return lax.all_to_all(value, 'col', split_axis=0, concat_axis=0, tiled=True)  31.5 us
    pallas_call x2, Pallas kernels, advance(): pl.pallas_call(functools.partial(advance_kernel, per_step), grid=(blocks...  30.7 us
    all_to_all x5, starting transfers between devices, exchanged(): return lax.all_to_all(value, 'col', split_axis=0, concat_axis=0, tiled=True)  29.6 us
    ppermute x12, starting transfers between devices, shifted(): return lax.ppermute(value, axis, pairs)  24.3 us
    dot_general x7, matrix products, rotated(): jnp.dot(cells, upper, preferred_element_type=jnp.float32)  17.9 us
    reshape x2, local copies, waits for them, and re-layouts, body(): far_weights = lax.dot_general(hit, got_weights, (((2,), (1,)), ((0,), (0,...  12.9 us
  transfers between devices with their start and end apart: 19, of which 3 were waited for; matrix products, arithmetic and copies ran while one was open for 10% of the time, Pallas kernels for 7%

profile of v1, /device:TPU:25, one launch (start us, length us, event | category | flops | bytes accessed | tf_op | source)
XLA Modules:
  0.0 506.3 jit_solution(717766687665969715)
XLA Ops:
  10.2 5.5 %all-to-all-start.1 = ((s32[8,1,8]{2,1,0:T(1,128)}), s32[8,1,8]{2,1,0:T(1,128)S(1)}, u32[]{:S(2)}, u32[]{:S(2)}) async-start(s32[8,1,8]{2,1,0:T(1,128)} %bitcast.9), calls=%async_computation.1 | async-start | bytes 8192 | tf_op jit(solution)/shard_map/all_to_all | solution.py:131
  15.6 3.4 fusion
  19.1 6.0 %all-to-all-start.2 = ((bf16[8,8,16384]{2,1,0:T(8,128)(2,1)}), bf16[8,8,16384]{2,1,0:T(8,128)(2,1)}, u32[]{:S(2)}, u32[]{:S(2)}) async-start(bf16[8,8,16384]{2,1,0:T(8,128)(2,1)} %fusion), calls=%async_computation.2 | async-start | bytes 4194304 | tf_op jit(solution)/shard_map/all_to_all | solution.py:131
  25.2 1.8 multiply_convert_fusion.4.own_ref
  27.0 5.4 %collective-permute-start.2 = (bf16[16,128,512]{2,1,0:T(8,128)(2,1)}, bf16[16,128,512]{2,1,0:T(8,128)(2,1)}, u32[]{:S(2)}, u32[]{:S(2)}) collective-permute-start(bf16[16,128,512]{2,1,0:T(8,128)(2,1)} %multiply_convert_fusion.4.own_ref), channel_id=1, source_target_pairs={{0,1},{1,2},{2,3},{4,5},{5,6},{6,7},{8,9},{9,10},{10,11},{12,13},{... | collective-permute-start | bytes 6291464 | tf_op jit(solution)/shard_map/ppermute | solution.py:119
  32.4 1.9 collective-permute-start.3
  37.8 1.9 collective-permute-start.11
  40.1 2.4 copy.41
  45.9 31.5 %all-to-all-done.2 = bf16[8,8,16384]{2,1,0:T(8,128)(2,1)} async-done(((bf16[8,8,16384]{2,1,0:T(8,128)(2,1)}), bf16[8,8,16384]{2,1,0:T(8,128)(2,1)}, u32[]{:S(2)}, u32[]{:S(2)}) %all-to-all-start.2) | async-done | bytes 2097184 | tf_op jit(solution)/shard_map/all_to_all | solution.py:131
  77.4 4.5 all-to-all-start
  82.1 1.4 copy.37
  83.5 1.3 copy.39
  86.4 1.6 maximum_maximum_fusion.1
  87.9 2.9 convolution_convert_fusion.2
  92.1 5.7 %copy.50 = bf16[8,16,128,128]{3,0,2,1:T(8,128)(2,1)} copy(bf16[8,16,128,128]{3,2,1,0:T(8,128)(2,1)S(1)} %bitcast.121) | data formatting | bytes 8388608 | tf_op jit(solution)/shard_map/reshape | solution.py:270
  97.8 7.3 %reshape.98.far_weights_ref = bf16[16,128,1024]{2,1,0:T(8,128)(2,1)} reshape(bf16[16,128,8,128]{3,2,1,0:T(8,128)(2,1)} %bitcast.122) | data formatting | bytes 8388608 | tf_op jit(solution)/shard_map/reshape | solution.py:272
  105.1 4.2 collective-permute-start.9
  110.3 5.4 %all-to-all-start.4 = ((f32[8,2,128]{2,1,0:T(2,128)}), f32[8,2,128]{2,1,0:T(2,128)S(1)}, u32[]{:S(2)}, u32[]{:S(2)}) async-start(f32[8,2,128]{2,1,0:T(2,128)} %select_reduce_fusion), calls=%async_computation.4 | async-start | bytes 16384 | tf_op jit(solution)/shard_map/all_to_all | solution.py:131
  120.1 15.3 %advance.2 = (bf16[16,128,512]{2,1,0:T(8,128)(2,1)S(1)}, f32[512,512]{1,0:T(8,128)}) custom-call(bf16[16,128,512]{2,1,0:T(8,128)(2,1)} %bitcast.115, bf16[2,128,512]{2,1,0:T(8,128)(2,1)S(1)} %collective-permute-done.before_ref, bf16[16,128,512]{2,1,0:T(8,128)(2,1)} %multiply_convert_fusion.4.own_ref, bf16[2,128,512]{2,1,0:T(8,128)(2,1)S(1)} %copy-done.6, ...), custom_call_target="tpu_custom_call" | custom-call | tf_op jit(solution)/shard_map/advance/pallas_call | solution.py:176
  138.3 8.2 %all-to-all-start.3 = ((bf16[8,128,512]{2,1,0:T(8,128)(2,1)}), bf16[8,128,512]{2,1,0:T(8,128)(2,1)}, u32[]{:S(2)}, u32[]{:S(2)}) async-start(bf16[8,128,512]{2,1,0:T(8,128)(2,1)} %copy.38), calls=%async_computation.3 | async-start | bytes 2097152 | tf_op jit(solution)/shard_map/all_to_all | solution.py:131
  146.5 1.9 collective-permute-start.10
  148.4 3.6 collective-permute-start.8
  154.4 135.9 %all-reduce.3.cloned.1.call-done.gram_ref = f32[512,512]{1,0:T(8,128)} async-done(((f32[512,512]{1,0:T(8,128)}), f32[512,512]{1,0:T(8,128)}) %all-reduce.3.cloned.1.call-update) | async-done | bytes 1048592 | tf_op jit(solution)/shard_map/psum | solution.py:300
  291.5 21.8 %orthonormalize.2 = (bf16[512,512]{1,0:T(8,128)(2,1)S(1)}, f32[1,512]{1,0:T(1,128)S(1)}) custom-call(f32[512,512]{1,0:T(8,128)S(1)} %copy-done.3), custom_call_target="tpu_custom_call" | custom-call | tf_op jit(solution)/shard_map/orthonormalize/pallas_call | solution.py:92
  314.9 3.3 multiply_convert_fusion.2
  318.1 1.9 multiply_convert_fusion.6
  320.1 4.2 multiply_convert_fusion.below_ref
  324.3 4.3 multiply_convert_fusion.1.above_ref
  328.6 15.4 %advance.3 = (bf16[16,128,512]{2,1,0:T(8,128)(2,1)S(1)}, f32[512,512]{1,0:T(8,128)}) custom-call(bf16[16,128,512]{2,1,0:T(8,128)(2,1)} %get-tuple-element.44.tangents_ref, bf16[2,128,512]{2,1,0:T(8,128)(2,1)S(1)} %fusion.6.before_ref, bf16[16,128,512]{2,1,0:T(8,128)(2,1)} %get-tuple-element.43.own_ref, bf16[2,128,512]{2,1,0:T(8,128)(2,1)S(1)} %fusion.3.after_ref, ...), custom_call_target="tpu_custom_call" | custom-call | tf_op jit(solution)/shard_map/advance/pallas_call | solution.py:176
  344.1 128.9 %all-reduce.5.cloned.1.call-done.gram_ref = f32[512,512]{1,0:T(8,128)} async-done(((f32[512,512]{1,0:T(8,128)}), f32[512,512]{1,0:T(8,128)}) %all-reduce.5.cloned.1.call-update) | async-done | bytes 1048592 | tf_op jit(solution)/shard_map/psum | solution.py:300
  474.2 22.0 %orthonormalize.3 = (bf16[512,512]{1,0:T(8,128)(2,1)S(1)}, f32[1,512]{1,0:T(1,128)S(1)}) custom-call(f32[512,512]{1,0:T(8,128)S(1)} %copy-done.4), custom_call_target="tpu_custom_call" | custom-call | tf_op jit(solution)/shard_map/orthonormalize/pallas_call | solution.py:92
  496.8 2.6 convert_bitcast_fusion
  (98 shorter events, 28.3 us)
Async XLA Ops:
  10.2 8.9 %all-to-all-start.1 = ((s32[8,1,8]{2,1,0:T(1,128)}), s32[8,1,8]{2,1,0:T(1,128)S(1)}, u32[]{:S(2)}, u32[]{:S(2)}) async-start(s32[8,1,8]{2,1,0:T(1,128)} %bitcast.9), calls=%async_computation.1 | async-start | bytes 8192 | tf_op jit(solution)/shard_map/all_to_all | solution.py:131
  19.1 6.1 %copy-start.11 = (f32[2,1,16,128]{3,2,1,0:T(8,128)S(1)}, f32[2,1,16,128]{3,2,1,0:T(8,128)}, u32[]{:S(2)}) copy-start(f32[2,1,16,128]{3,2,1,0:T(8,128)} %param.10) | copy-start | bytes 49156
  19.1 6.1 %copy-start.7 = (bf16[1,16,128,512]{3,2,1,0:T(8,128)(2,1)S(1)}, bf16[1,16,128,512]{3,2,1,0:T(8,128)(2,1)}, u32[]{:S(2)}) copy-start(bf16[1,16,128,512]{3,2,1,0:T(8,128)(2,1)} %param.9) | copy-start | bytes 6291460
  19.1 58.3 %all-to-all-start.2 = ((bf16[8,8,16384]{2,1,0:T(8,128)(2,1)}), bf16[8,8,16384]{2,1,0:T(8,128)(2,1)}, u32[]{:S(2)}, u32[]{:S(2)}) async-start(bf16[8,8,16384]{2,1,0:T(8,128)(2,1)} %fusion), calls=%async_computation.2 | async-start | bytes 4194304 | tf_op jit(solution)/shard_map/all_to_all | solution.py:131
  27.0 90.6 %collective-permute-start.2 = (bf16[16,128,512]{2,1,0:T(8,128)(2,1)}, bf16[16,128,512]{2,1,0:T(8,128)(2,1)}, u32[]{:S(2)}, u32[]{:S(2)}) collective-permute-start(bf16[16,128,512]{2,1,0:T(8,128)(2,1)} %multiply_convert_fusion.4.own_ref), channel_id=1, source_target_pairs={{0,1},{1,2},{2,3},{4,5},{5,6},{6,7},{8,9},{9,10},{10,11},{12,13},{... | collective-permute-start | bytes 6291464 | tf_op jit(solution)/shard_map/ppermute | solution.py:119
  32.4 85.5 %collective-permute-start.3 = (bf16[16,128,512]{2,1,0:T(8,128)(2,1)}, bf16[16,128,512]{2,1,0:T(8,128)(2,1)}, u32[]{:S(2)}, u32[]{:S(2)}) collective-permute-start(bf16[16,128,512]{2,1,0:T(8,128)(2,1)} %multiply_convert_fusion.4.own_ref), channel_id=1, source_target_pairs={{1,0},{2,1},{3,2},{5,4},{6,5},{7,6},{9,8},{10,9},{11,10},{13,12},{... | collective-permute-start | bytes 6291464 | tf_op jit(solution)/shard_map/ppermute | solution.py:119
  35.4 69.7 %collective-permute-start = (bf16[2,128,512]{2,1,0:T(8,128)(2,1)S(1)}, bf16[2,128,512]{2,1,0:T(8,128)(2,1)S(1)}, u32[]{:S(2)}, u32[]{:S(2)}) collective-permute-start(bf16[2,128,512]{2,1,0:T(8,128)(2,1)S(1)} %get-tuple-element.21), channel_id=1, source_target_pairs={{0,4},{4,8},{8,12},{12,16},{16,20},{20,24},{24,28},{28,0},{1,5},{5... | collective-permute-start | bytes 786440 | tf_op jit(solution)/shard_map/ppermute | solution.py:119
  36.6 79.1 %collective-permute-start.1 = (bf16[2,128,512]{2,1,0:T(8,128)(2,1)S(1)}, bf16[2,128,512]{2,1,0:T(8,128)(2,1)S(1)}, u32[]{:S(2)}, u32[]{:S(2)}) collective-permute-start(bf16[2,128,512]{2,1,0:T(8,128)(2,1)S(1)} %get-tuple-element.20), channel_id=1, source_target_pairs={{0,28},{4,0},{8,4},{12,8},{16,12},{20,16},{24,20},{28,24},{1,29},{... | collective-permute-start | bytes 786440 | tf_op jit(solution)/shard_map/ppermute | solution.py:119
  37.8 116.3 %collective-permute-start.11 = (f32[16,2,128]{2,0,1:T(8,128)S(1)}, f32[16,2,128]{2,0,1:T(8,128)S(1)}, u32[]{:S(2)}, u32[]{:S(2)}) collective-permute-start(f32[16,2,128]{2,0,1:T(8,128)S(1)} %fusion.39), channel_id=1, source_target_pairs={{1,0},{2,1},{3,2},{5,4},{6,5},{7,6},{9,8},{10,9},{11,10},{13,12},{... | collective-permute-start | bytes 49160 | tf_op jit(solution)/shard_map/ppermute | solution.py:119
  40.1 2.5 copy-start.8
  42.5 1.3 copy-start.13
  42.5 1.3 copy-start.12
  42.6 1.3 copy-start.14
  77.4 31.9 %all-to-all-start = ((bf16[8,128,512]{2,1,0:T(8,128)(2,1)}), bf16[8,128,512]{2,1,0:T(8,128)(2,1)S(1)}, u32[]{:S(2)}, u32[]{:S(2)}) async-start(bf16[8,128,512]{2,1,0:T(8,128)(2,1)} %copy.33), calls=%async_computation | async-start | bytes 2097152 | tf_op jit(solution)/shard_map/all_to_all | solution.py:131
  84.8 1.5 copy-start.9
  84.8 1.5 copy-start.10
  105.1 49.3 %collective-permute-start.9 = (f32[16,2,128]{2,0,1:T(8,128)S(1)}, f32[16,2,128]{2,0,1:T(8,128)S(1)}, u32[]{:S(2)}, u32[]{:S(2)}) collective-permute-start(f32[16,2,128]{2,0,1:T(8,128)S(1)} %fusion.39), channel_id=1, source_target_pairs={{0,1},{1,2},{2,3},{4,5},{5,6},{6,7},{8,9},{9,10},{10,11},{12,13},{... | collective-permute-start | bytes 49160 | tf_op jit(solution)/shard_map/ppermute | solution.py:119
  109.3 1.0 copy-start.1
  110.3 28.0 %all-to-all-start.4 = ((f32[8,2,128]{2,1,0:T(2,128)}), f32[8,2,128]{2,1,0:T(2,128)S(1)}, u32[]{:S(2)}, u32[]{:S(2)}) async-start(f32[8,2,128]{2,1,0:T(2,128)} %select_reduce_fusion), calls=%async_computation.4 | async-start | bytes 16384 | tf_op jit(solution)/shard_map/all_to_all | solution.py:131
  116.4 30.0 %collective-permute-start.7 = (f32[2,2,128]{2,0,1:T(2,128)S(1)}, f32[2,2,128]{2,0,1:T(2,128)S(1)}, u32[]{:S(2)}, u32[]{:S(2)}) collective-permute-start(f32[2,2,128]{2,0,1:T(2,128)S(1)} %get-tuple-element.26), channel_id=1, source_target_pairs={{0,28},{4,0},{8,4},{12,8},{16,12},{20,16},{24,20},{28,24},{1,29},{... | collective-permute-start | bytes 6152 | tf_op jit(solution)/shard_map/ppermute | solution.py:119
  117.6 30.8 %collective-permute-start.5 = (f32[2,2,128]{2,0,1:T(2,128)S(1)}, f32[2,2,128]{2,0,1:T(2,128)S(1)}, u32[]{:S(2)}, u32[]{:S(2)}) collective-permute-start(f32[2,2,128]{2,0,1:T(2,128)S(1)} %get-tuple-element.27), channel_id=1, source_target_pairs={{0,4},{4,8},{8,12},{12,16},{16,20},{20,24},{24,28},{28,0},{1,5},{5... | collective-permute-start | bytes 6152 | tf_op jit(solution)/shard_map/ppermute | solution.py:119
  117.9 1.2 copy-start.2
  138.3 179.8 %all-to-all-start.3 = ((bf16[8,128,512]{2,1,0:T(8,128)(2,1)}), bf16[8,128,512]{2,1,0:T(8,128)(2,1)}, u32[]{:S(2)}, u32[]{:S(2)}) async-start(bf16[8,128,512]{2,1,0:T(8,128)(2,1)} %copy.38), calls=%async_computation.3 | async-start | bytes 2097152 | tf_op jit(solution)/shard_map/all_to_all | solution.py:131
  146.4 143.8 %all-reduce.3.cloned.1.call-start = ((), (), s32[]{:S(2)}) async-start(), calls=%async_computation.5 | async-start | bytes 2097152 | tf_op jit(solution)/shard_map/psum | solution.py:300
  146.5 173.6 %collective-permute-start.10 = (bf16[16,128,512]{2,1,0:T(8,128)(2,1)S(1)}, bf16[16,128,512]{2,1,0:T(8,128)(2,1)}, u32[]{:S(2)}, u32[]{:S(2)}) collective-permute-start(bf16[16,128,512]{2,1,0:T(8,128)(2,1)S(1)} %get-tuple-element.10), channel_id=1, source_target_pairs={{1,0},{2,1},{3,2},{5,4},{6,5},{7,6},{9,8},{10,9},{11,10},{13,12},{... | collective-permute-start | bytes 6291464 | tf_op jit(solution)/shard_map/ppermute | solution.py:119
  148.4 175.9 %collective-permute-start.8 = (bf16[16,128,512]{2,1,0:T(8,128)(2,1)S(1)}, bf16[16,128,512]{2,1,0:T(8,128)(2,1)}, u32[]{:S(2)}, u32[]{:S(2)}) collective-permute-start(bf16[16,128,512]{2,1,0:T(8,128)(2,1)S(1)} %get-tuple-element.10), channel_id=1, source_target_pairs={{0,1},{1,2},{2,3},{4,5},{5,6},{6,7},{8,9},{9,10},{10,11},{12,13},{... | collective-permute-start | bytes 6291464 | tf_op jit(solution)/shard_map/ppermute | solution.py:119
  152.1 320.9 %all-reduce.5.cloned.1.call-start = ((), (), s32[]{:S(2)}) async-start(), calls=%async_computation.6 | async-start | bytes 2097152 | tf_op jit(solution)/shard_map/psum | solution.py:300
  152.9 160.4 %collective-permute-start.6 = (bf16[2,128,512]{2,1,0:T(8,128)(2,1)S(1)}, bf16[2,128,512]{2,1,0:T(8,128)(2,1)S(1)}, u32[]{:S(2)}, u32[]{:S(2)}) collective-permute-start(bf16[2,128,512]{2,1,0:T(8,128)(2,1)S(1)} %get-tuple-element.18), channel_id=1, source_target_pairs={{0,28},{4,0},{8,4},{12,8},{16,12},{20,16},{24,20},{28,24},{1,29},{... | collective-permute-start | bytes 786440 | tf_op jit(solution)/shard_map/ppermute | solution.py:119
  154.1 159.5 %collective-permute-start.4 = (bf16[2,128,512]{2,1,0:T(8,128)(2,1)}, bf16[2,128,512]{2,1,0:T(8,128)(2,1)}, u32[]{:S(2)}, u32[]{:S(2)}) collective-permute-start(bf16[2,128,512]{2,1,0:T(8,128)(2,1)} %get-tuple-element.19), channel_id=1, source_target_pairs={{0,4},{4,8},{8,12},{12,16},{16,20},{20,24},{24,28},{28,0},{1,5},{5... | collective-permute-start | bytes 786440 | tf_op jit(solution)/shard_map/ppermute | solution.py:119
  290.3 1.2 copy-start.3
  324.3 4.3 copy-start
  473.0 1.2 copy-start.4
  (2 other events, 1.7 us)
Sparse Core Ops, SparseCore 0:
  152.4 137.7 all-reduce.2
  344.2 128.7 all-reduce.4

commit v2 on v1

--- a/solution.py
+++ b/solution.py
@@ -15,6 +15,138 @@
 HI = lax.Precision.HIGHEST
 NB = 128
 ROWS = 8
+MESH = pl.DeviceIdType.MESH
+LANES = 128
+
+
+def half_rows(vectors, chunks):
+    count = -(-vectors // LANES)
+    rows = -(-(count * (count + 1) // 2) // 2) * LANES
+    return -(-rows // (8 * chunks)) * 8 * chunks
+
+
+def packed_places(vectors, half):
+    count = -(-vectors // LANES)
+    pairs = [(i, j) for i in range(count) for j in range(i + 1)]
+    each = -(-len(pairs) // 2)
+    return [(i, j, (k // each) * half + (k % each) * LANES) for k, (i, j) in enumerate(pairs)]
+
+
+def sum_kernel(groups, per_col, packed_ref, total_ref, mate_in, part, arrived, sems):
+    chunk = part.shape[1]
+    half = groups * chunk
+    col, layer = lax.axis_index("col"), lax.axis_index("layer")
+    core = lax.rem(layer, 2)
+    mate = {"col": col, "layer": layer + 1 - 2 * core}
+    me = col * per_col + layer // 2
+
+    def peer(step):
+        k = lax.rem(me + step, groups)
+        return k, {"col": k // per_col, "layer": lax.rem(k, per_col) * 2 + core}
+
+    def remote(source, target, kind, sent, got, device):
+        return pltpu.make_async_remote_copy(
+            src_ref=source,
+            dst_ref=target,
+            send_sem=sems.at[kind, sent],
+            recv_sem=sems.at[kind + 1, got],
+            device_id=device,
+            device_id_type=MESH,
+        )
+
+    barrier = pltpu.get_barrier_semaphore()
+    pl.semaphore_signal(barrier, inc=1, device_id=mate, device_id_type=MESH)
+
+    def greet(step, carry):
+        _, device = peer(step)
+        pl.semaphore_signal(barrier, inc=1, device_id=device, device_id_type=MESH)
+        return carry
+
+    lax.fori_loop(1, groups, greet, 0)
+    pl.semaphore_wait(barrier, groups)
+
+    mine = pl.multiple_of(core * half, 8)
+    other = pl.multiple_of((1 - core) * half, 8)
+    swap = remote(packed_ref.at[pl.ds(other, half)], mate_in, 6, 0, 0, mate)
+    swap.start()
+    swap.wait()
+    part[...] = (packed_ref[pl.ds(mine, half), :] + mate_in[...]).reshape(part.shape)
+
+    def scatter(step, carry):
+        k, device = peer(step)
+        remote(part.at[k], arrived.at[me], 0, k, me, device).start()
+        return carry
+
+    def scattered(step, carry):
+        k, device = peer(step)
+        copy = remote(part.at[k], arrived.at[k], 0, k, k, device)
+        copy.wait_send()
+        copy.wait_recv()
+        return carry
+
+    lax.fori_loop(1, groups, scatter, 0)
+    arrived[me] = part[me]
+    lax.fori_loop(1, groups, scattered, 0)
+
+    def place(k):
+        return total_ref.at[pl.ds(pl.multiple_of(core * half + k * chunk, 8), chunk)]
+
+    def mate_place(k):
+        return total_ref.at[pl.ds(pl.multiple_of((1 - core) * half + k * chunk, 8), chunk)]
+
+    place(me)[...] = jnp.sum(arrived[...], axis=0)
+
+    def spread(step, carry):
+        k, device = peer(step)
+        remote(place(me), place(me), 2, k, me, device).start()
+        return carry
+
+    def forward(step, carry):
+        k, device = peer(step)
+        copy = remote(place(me), place(k), 2, k, k, device)
+        copy.wait_recv()
+        remote(place(k), place(k), 4, k, k, mate).start()
+        return carry
+
+    def finish(step, carry):
+        k, device = peer(step)
+        remote(place(me), place(k), 2, k, k, device).wait_send()
+        copy = remote(place(k), mate_place(k), 4, k, k, mate)
+        copy.wait_send()
+        copy.wait_recv()
+        return carry
+
+    lax.fori_loop(1, groups, spread, 0)
+    own = remote(place(me), place(me), 4, me, me, mate)
+    own.start()
+    lax.fori_loop(1, groups, forward, 0)
+    last = remote(place(me), mate_place(me), 4, me, me, mate)
+    last.wait_send()
+    last.wait_recv()
+    lax.fori_loop(1, groups, finish, 0)
+
+
+def summed(packed):
+    per_col = lax.axis_size("layer") // 2
+    groups = lax.axis_size("col") * per_col
+    half = packed.shape[0] // 2
+    chunk = half // groups
+    return pl.pallas_call(
+        functools.partial(sum_kernel, groups, per_col),
+        out_shape=jax.ShapeDtypeStruct(packed.shape, packed.dtype),
+        in_specs=[pl.BlockSpec(memory_space=pltpu.VMEM)],
+        out_specs=pl.BlockSpec(memory_space=pltpu.VMEM),
+        scratch_shapes=[
+            pltpu.VMEM((half, LANES), packed.dtype),
+            pltpu.VMEM((groups, chunk, LANES), packed.dtype),
+            pltpu.VMEM((groups, chunk, LANES), packed.dtype),
+            pltpu.SemaphoreType.DMA((8, groups)),
+        ],
+        compiler_params=pltpu.CompilerParams(
+            collective_id=0, has_side_effects=True, vmem_limit_bytes=16 * 1024 * 1024
+        ),
+        name="sum_gram",
+    )(packed)
 
 
 def inverse_factor(block):
@@ -60,9 +192,13 @@
     return jnp.where(rows_id >= cols_id, out, 0.0)
 
 
-def orthonormal_kernel(count, gram_ref, upper_ref, growth_ref, work):
-    n = gram_ref.shape[0]
-    work[...] = gram_ref[...] * (1.0 / count)
+def orthonormal_kernel(count, packed_ref, upper_ref, growth_ref, work):
+    n = upper_ref.shape[0]
+    for i, j, at in packed_places(n, packed_ref.shape[0] // 2):
+        block = packed_ref[at : at + LANES] * (1.0 / count)
+        work[i * LANES : (i + 1) * LANES, j * LANES : (j + 1) * LANES] = block
+        if i > j:
+            work[j * LANES : (j + 1) * LANES, i * LANES : (i + 1) * LANES] = block.T
     cols_id = lax.broadcasted_iota(jnp.int32, (NB, n), 1)
 
     def step(i, carry):
@@ -87,8 +223,7 @@
     growth_ref[...] = -jnp.log(jnp.sum(jnp.where(rows_n == cols_n, full, 0.0), axis=0, keepdims=True))
 
 
-def orthonormalize(gram_total, count):
-    n = gram_total.shape[0]
+def orthonormalize(gram_total, count, n):
     upper, growth = pl.pallas_call(
         functools.partial(orthonormal_kernel, count),
         out_shape=(
@@ -133,7 +268,7 @@
 
 def advance_kernel(
     per_step, tangents_ref, before_ref, own_ref, after_ref, above_ref, below_ref, far_ref,
-    weights_ref, far_weights_ref, coef_ref, advanced_ref, gram_ref, wide
+    weights_ref, far_weights_ref, coef_ref, advanced_ref, gram_ref, wide, total
 ):
     index = pl.program_id(0)
     blocks, size, _ = own_ref.shape
@@ -143,7 +278,7 @@
         wide[0:2] = before_ref[...]
         wide[2 : 2 + blocks] = own_ref[...]
         wide[2 + blocks : 4 + blocks] = after_ref[...]
-        gram_ref[...] = jnp.zeros_like(gram_ref)
+        total[...] = jnp.zeros_like(total)
 
     for k in range(per_step):
         at = index * per_step + k
@@ -160,13 +295,22 @@
         now = tangents_ref[k].astype(jnp.float32)
         advanced_ref[k] = (now + TIME_STEP * (drive - coef[:, 8:9] * now)).astype(jnp.bfloat16)
     rows = advanced_ref[...].reshape(per_step * size, advanced_ref.shape[-1])
-    gram_ref[...] += lax.dot_general(
+    total[...] += lax.dot_general(
         rows, rows, (((0,), (0,)), ((), ())), preferred_element_type=jnp.float32
     )
+
+    @pl.when(index == pl.num_programs(0) - 1)
+    def _():
+        gram_ref[...] = jnp.zeros_like(gram_ref)
+        for i, j, at in packed_places(total.shape[0], gram_ref.shape[0] // 2):
+            gram_ref[at : at + LANES] = total[
+                i * LANES : (i + 1) * LANES, j * LANES : (j + 1) * LANES
+            ]
 
 
 def advance(tangents, before, own, after, above, below, far, weights, far_weights, coef):
     blocks, size, vectors = tangents.shape
+    half = half_rows(vectors, lax.axis_size("col") * lax.axis_size("layer") // 2)
     per_step = 2 if blocks % 2 == 0 else 1
     whole = pl.BlockSpec(memory_space=pltpu.VMEM)
 
@@ -178,7 +322,7 @@
         grid=(blocks // per_step,),
         out_shape=(
             jax.ShapeDtypeStruct(tangents.shape, jnp.bfloat16),
-            jax.ShapeDtypeStruct((vectors, vectors), jnp.float32),
+            jax.ShapeDtypeStruct((2 * half, LANES), jnp.float32),
         ),
         in_specs=[
             split(size, vectors),
@@ -187,8 +331,11 @@
             split(size, far.shape[0]),
             split(size, coef.shape[-1]),
         ],
-        out_specs=(split(size, vectors), pl.BlockSpec((vectors, vectors), lambda i: (0, 0))),
-        scratch_shapes=[pltpu.VMEM((blocks + 4, size, vectors), jnp.bfloat16)],
+        out_specs=(split(size, vectors), pl.BlockSpec((2 * half, LANES), lambda i: (0, 0))),
+        scratch_shapes=[
+            pltpu.VMEM((blocks + 4, size, vectors), jnp.bfloat16),
+            pltpu.VMEM((vectors, vectors), jnp.float32),
+        ],
         compiler_params=pltpu.CompilerParams(
             vmem_limit_bytes=48 * 1024 * 1024, dimension_semantics=("arbitrary",)
         ),
@@ -297,12 +444,12 @@
             state, edges[0], scaled, edges[1], edges[2], edges[3],
             far.reshape(col_count * size, vectors), local_weights[0], far_weights, coef,
         )
-        gram = lax.psum(gram, ("col", "layer"))
+        gram = summed(gram)
         last = t == steps - 1
         if not last:
             edges = neighbours(advanced)
             far = exchanged(bundle(advanced))
-        upper, grown = orthonormalize(gram, neurons)
+        upper, grown = orthonormalize(gram, neurons, vectors)
         growth = growth + grown
 
         def rotated(cells):

time: 512 us -> 297 us (0.58)
  waiting for transfers between devices: 296 us -> 40.2 us
  Pallas kernels: 74.5 us -> 138 us
  between operations: 14.4 us -> 1.1 us
    psum x2 -> x0, waiting for transfers between devices: 265 us -> none  [body(): gram = lax.psum(gram, ('col', 'layer'))]
    pallas_call x0 -> x2, Pallas kernels: none -> 65.3 us  [summed(): pl.pallas_call(functools.partial(sum_kernel, groups, per_col), out_shape=...]
    ppermute x12, waiting for transfers between devices: 0.03 us -> 8.68 us  [shifted(): return lax.ppermute(value, axis, pairs)]
  transfers between devices with their start and end apart: 19 -> 17, of which waited for: 3 -> 2; matrix products, arithmetic and copies ran while one was open for 10% -> 16% of each run, Pallas kernels for 7% -> 25%
where the time goes in v2:
time: 297 us; the launch traced here: 296 us
  Pallas kernels  138 us (46%)
  starting transfers between devices  54.2 us (18%)
  waiting for transfers between devices  40.2 us (14%)
  local copies, waits for them, and re-layouts  30.7 us (10%)
  matrix products  24.4 us (8%)
  other arithmetic  7.76 us (3%)
    pallas_call x2, Pallas kernels, summed(): pl.pallas_call(functools.partial(sum_kernel, groups, per_col), out_shape=...  65.3 us
    pallas_call x2, Pallas kernels, orthonormalize(): pl.pallas_call(functools.partial(orthonormal_kernel, count), out_shape=(j...  43.8 us
    all_to_all x5, waiting for transfers between devices, exchanged(): return lax.all_to_all(value, 'col', split_axis=0, concat_axis=0, tiled=True)  31.5 us
    all_to_all x5, starting transfers between devices, exchanged(): return lax.all_to_all(value, 'col', split_axis=0, concat_axis=0, tiled=True)  29.6 us
    pallas_call x2, Pallas kernels, advance(): pl.pallas_call(functools.partial(advance_kernel, per_step), grid=(blocks...  28.9 us
    ppermute x12, starting transfers between devices, shifted(): return lax.ppermute(value, axis, pairs)  24.6 us
    dot_general x7, matrix products, rotated(): jnp.dot(cells, upper, preferred_element_type=jnp.float32)  16.9 us
    reshape x2, local copies, waits for them, and re-layouts, body(): far_weights = lax.dot_general(hit, got_weights, (((2,), (1,)), ((0,), (0,...  12.9 us
  transfers between devices with their start and end apart: 17, of which 2 were waited for; matrix products, arithmetic and copies ran while one was open for 16% of the time, Pallas kernels for 25%

profile of v2, /device:TPU:25, one launch (start us, length us, event | category | flops | bytes accessed | tf_op | source)
XLA Modules:
  0.0 296.3 jit_solution(5264139705786719359)
XLA Ops:
  3.6 5.5 %all-to-all-start.1 = ((s32[8,1,8]{2,1,0:T(1,128)}), s32[8,1,8]{2,1,0:T(1,128)S(1)}, u32[]{:S(2)}, u32[]{:S(2)}) async-start(s32[8,1,8]{2,1,0:T(1,128)} %bitcast.9), calls=%async_computation.1 | async-start | bytes 8192 | tf_op jit(solution)/shard_map/all_to_all | solution.py:266
  9.1 3.4 %fusion = bf16[8,8,16384]{2,1,0:T(8,128)(2,1)} fusion(bf16[4,8,128,128]{3,2,1,0:T(8,128)(2,1)} %bitcast.128, s32[32]{0:T(128)S(1)} %multiply_add_fusion), kind=kOutput, calls=%fused_computation.4 | convolution fusion | flops 68159488 | bytes 3145856 | tf_op jit(solution)/shard_map/dot_general | solution.py:379
  12.5 6.0 %all-to-all-start.2 = ((bf16[8,8,16384]{2,1,0:T(8,128)(2,1)}), bf16[8,8,16384]{2,1,0:T(8,128)(2,1)}, u32[]{:S(2)}, u32[]{:S(2)}) async-start(bf16[8,8,16384]{2,1,0:T(8,128)(2,1)} %fusion), calls=%async_computation.2 | async-start | bytes 4194304 | tf_op jit(solution)/shard_map/all_to_all | solution.py:266
  18.6 1.8 multiply_convert_fusion.4.own_ref
  20.4 5.4 %collective-permute-start.2 = (bf16[16,128,512]{2,1,0:T(8,128)(2,1)}, bf16[16,128,512]{2,1,0:T(8,128)(2,1)}, u32[]{:S(2)}, u32[]{:S(2)}) collective-permute-start(bf16[16,128,512]{2,1,0:T(8,128)(2,1)} %multiply_convert_fusion.4.own_ref), channel_id=1, source_target_pairs={{0,1},{1,2},{2,3},{4,5},{5,6},{6,7},{8,9},{9,10},{10,11},{12,13},{... | collective-permute-start | bytes 6291464 | tf_op jit(solution)/shard_map/ppermute | solution.py:254
  25.8 1.9 collective-permute-start.3
  31.3 1.9 collective-permute-start.11
  33.6 2.4 copy.41
  39.4 31.5 %all-to-all-done.2 = bf16[8,8,16384]{2,1,0:T(8,128)(2,1)} async-done(((bf16[8,8,16384]{2,1,0:T(8,128)(2,1)}), bf16[8,8,16384]{2,1,0:T(8,128)(2,1)}, u32[]{:S(2)}, u32[]{:S(2)}) %all-to-all-start.2) | async-done | bytes 2097184 | tf_op jit(solution)/shard_map/all_to_all | solution.py:266
  70.9 4.5 %all-to-all-start = ((bf16[8,128,512]{2,1,0:T(8,128)(2,1)}), bf16[8,128,512]{2,1,0:T(8,128)(2,1)S(1)}, u32[]{:S(2)}, u32[]{:S(2)}) async-start(bf16[8,128,512]{2,1,0:T(8,128)(2,1)} %copy.33), calls=%async_computation | async-start | bytes 2097152 | tf_op jit(solution)/shard_map/all_to_all | solution.py:266
  79.8 1.6 maximum_maximum_fusion.1
  81.4 2.9 convolution_convert_fusion.2
  85.6 5.7 %copy.50 = bf16[8,16,128,128]{3,0,2,1:T(8,128)(2,1)} copy(bf16[8,16,128,128]{3,2,1,0:T(8,128)(2,1)S(1)} %bitcast.121) | data formatting | bytes 8388608 | tf_op jit(solution)/shard_map/reshape | solution.py:417
  91.3 7.3 %reshape.98.far_weights_ref = bf16[16,128,1024]{2,1,0:T(8,128)(2,1)} reshape(bf16[16,128,8,128]{3,2,1,0:T(8,128)(2,1)} %bitcast.122) | data formatting | bytes 8388608 | tf_op jit(solution)/shard_map/reshape | solution.py:419
  98.6 4.2 %collective-permute-start.9 = (f32[16,2,128]{2,0,1:T(8,128)S(1)}, f32[16,2,128]{2,0,1:T(8,128)S(1)}, u32[]{:S(2)}, u32[]{:S(2)}) collective-permute-start(f32[16,2,128]{2,0,1:T(8,128)S(1)} %fusion.39), channel_id=1, source_target_pairs={{0,1},{1,2},{2,3},{4,5},{5,6},{6,7},{8,9},{9,10},{10,11},{12,13},{... | collective-permute-start | bytes 49160 | tf_op jit(solution)/shard_map/ppermute | solution.py:254
  103.7 5.4 %all-to-all-start.4 = ((f32[8,2,128]{2,1,0:T(2,128)}), f32[8,2,128]{2,1,0:T(2,128)S(1)}, u32[]{:S(2)}, u32[]{:S(2)}) async-start(f32[8,2,128]{2,1,0:T(2,128)} %select_reduce_fusion), calls=%async_computation.4 | async-start | bytes 16384 | tf_op jit(solution)/shard_map/all_to_all | solution.py:266
  113.5 14.4 %advance.2 = (bf16[16,128,512]{2,1,0:T(8,128)(2,1)S(1)}, f32[1280,128]{1,0:T(8,128)S(1)}) custom-call(bf16[16,128,512]{2,1,0:T(8,128)(2,1)} %bitcast.115, bf16[2,128,512]{2,1,0:T(8,128)(2,1)S(1)} %collective-permute-done.before_ref, bf16[16,128,512]{2,1,0:T(8,128)(2,1)} %multiply_convert_fusion.4.own_ref, bf16[2,128,512]{2,1,0:T(8,128)(2,1)S(1)} %copy-done.6, ...), custom_call_target="tpu_custom_call" | custom-call | tf_op jit(solution)/shard_map/advance/pallas_call | solution.py:320
  130.9 8.1 %all-to-all-start.3 = ((bf16[8,128,512]{2,1,0:T(8,128)(2,1)}), bf16[8,128,512]{2,1,0:T(8,128)(2,1)}, u32[]{:S(2)}, u32[]{:S(2)}) async-start(bf16[8,128,512]{2,1,0:T(8,128)(2,1)} %copy.38), calls=%async_computation.3 | async-start | bytes 2097152 | tf_op jit(solution)/shard_map/all_to_all | solution.py:266
  139.0 1.9 collective-permute-start.10
  141.0 3.9 %collective-permute-start.8 = (bf16[16,128,512]{2,1,0:T(8,128)(2,1)S(1)}, bf16[16,128,512]{2,1,0:T(8,128)(2,1)}, u32[]{:S(2)}, u32[]{:S(2)}) collective-permute-start(bf16[16,128,512]{2,1,0:T(8,128)(2,1)S(1)} %get-tuple-element.10), channel_id=1, source_target_pairs={{0,1},{1,2},{2,3},{4,5},{5,6},{6,7},{8,9},{9,10},{10,11},{12,13},{... | collective-permute-start | bytes 6291464 | tf_op jit(solution)/shard_map/ppermute | solution.py:254
  144.9 38.8 %sum_gram.2.packed_ref = f32[1280,128]{1,0:T(8,128)S(1)} custom-call(f32[1280,128]{1,0:T(8,128)S(1)} %copy-done.4), custom_call_target="tpu_custom_call" | custom-call | tf_op jit(solution)/shard_map/sum_gram/pallas_call | solution.py:134
  183.7 21.9 %orthonormalize.2 = (bf16[512,512]{1,0:T(8,128)(2,1)S(1)}, f32[1,512]{1,0:T(1,128)S(1)}) custom-call(f32[1280,128]{1,0:T(8,128)S(1)} %sum_gram.2.packed_ref), custom_call_target="tpu_custom_call" | custom-call | tf_op jit(solution)/shard_map/orthonormalize/pallas_call | solution.py:227
  205.8 1.5 collective-permute-start.4
  207.2 3.3 %multiply_convert_fusion.2 = (bf16[16,128,512]{2,1,0:T(8,128)(2,1)}, bf16[16,128,512]{2,1,0:T(8,128)(2,1)}) fusion(f32[16,128]{1,0:T(8,128)S(1)} %get-tuple-element.28, bf16[16,128,512]{2,1,0:T(8,128)(2,1)S(1)} %get-tuple-element.10, bf16[512,512]{1,0:T(8,128)(2,1)S(1)} %get-tuple-element.12), kind=kOutput, calls=%fused_computation.8 | convolution fusion | flops 1077936128 | bytes 6823936 | tf_op jit(solution)/shard_map/dot_general | solution.py:456
  210.5 8.7 %collective-permute-done.6 = bf16[2,128,512]{2,1,0:T(8,128)(2,1)S(1)} collective-permute-done((bf16[2,128,512]{2,1,0:T(8,128)(2,1)S(1)}, bf16[2,128,512]{2,1,0:T(8,128)(2,1)S(1)}, u32[]{:S(2)}, u32[]{:S(2)}) %collective-permute-start.6) | collective-permute-done | bytes 262176 | tf_op jit(solution)/shard_map/ppermute | solution.py:254
  219.8 1.9 multiply_convert_fusion.6
  221.7 4.2 %multiply_convert_fusion.below_ref = bf16[16,128,512]{2,1,0:T(8,128)(2,1)} fusion(f32[16,128]{1,0:T(8,128)S(1)} %slice_bitcast_fusion, bf16[16,128,512]{2,1,0:T(8,128)(2,1)} %collective-permute-done.10, bf16[512,512]{1,0:T(8,128)(2,1)S(1)} %get-tuple-element.12), kind=kOutput, calls=%fused_computation.6 | convolution fusion | flops 1077936128 | bytes 4726784 | tf_op jit(solution)/shard_map/dot_general | solution.py:456
  225.9 4.3 %multiply_convert_fusion.1.above_ref = bf16[16,128,512]{2,1,0:T(8,128)(2,1)} fusion(f32[16,128]{1,0:T(8,128)S(1)} %slice_bitcast_fusion.1, bf16[16,128,512]{2,1,0:T(8,128)(2,1)} %collective-permute-done.8, bf16[512,512]{1,0:T(8,128)(2,1)S(1)} %get-tuple-element.12), kind=kOutput, calls=%fused_computation.7 | convolution fusion | flops 1077936128 | bytes 4726784 | tf_op jit(solution)/shard_map/dot_general | solution.py:456
  230.2 14.5 %advance.3 = (bf16[16,128,512]{2,1,0:T(8,128)(2,1)S(1)}, f32[1280,128]{1,0:T(8,128)S(1)}) custom-call(bf16[16,128,512]{2,1,0:T(8,128)(2,1)} %get-tuple-element.44.tangents_ref, bf16[2,128,512]{2,1,0:T(8,128)(2,1)S(1)} %fusion.6.before_ref, bf16[16,128,512]{2,1,0:T(8,128)(2,1)} %get-tuple-element.43.own_ref, bf16[2,128,512]{2,1,0:T(8,128)(2,1)S(1)} %fusion.3.after_ref, ...), custom_call_target="tpu_custom_call" | custom-call | tf_op jit(solution)/shard_map/advance/pallas_call | solution.py:320
  244.7 26.5 %sum_gram.3.packed_ref = f32[1280,128]{1,0:T(8,128)S(1)} custom-call(f32[1280,128]{1,0:T(8,128)S(1)} %get-tuple-element.14.packed_ref), custom_call_target="tpu_custom_call" | custom-call | tf_op jit(solution)/shard_map/sum_gram/pallas_call | solution.py:134
  271.2 21.9 %orthonormalize.3 = (bf16[512,512]{1,0:T(8,128)(2,1)S(1)}, f32[1,512]{1,0:T(1,128)S(1)}) custom-call(f32[1280,128]{1,0:T(8,128)S(1)} %sum_gram.3.packed_ref), custom_call_target="tpu_custom_call" | custom-call | tf_op jit(solution)/shard_map/orthonormalize/pallas_call | solution.py:227
  293.7 2.6 convert_bitcast_fusion
  (94 shorter events, 25.4 us)
Async XLA Ops:
  3.6 8.9 %all-to-all-start.1 = ((s32[8,1,8]{2,1,0:T(1,128)}), s32[8,1,8]{2,1,0:T(1,128)S(1)}, u32[]{:S(2)}, u32[]{:S(2)}) async-start(s32[8,1,8]{2,1,0:T(1,128)} %bitcast.9), calls=%async_computation.1 | async-start | bytes 8192 | tf_op jit(solution)/shard_map/all_to_all | solution.py:266
  12.5 6.1 %copy-start.11 = (f32[2,1,16,128]{3,2,1,0:T(8,128)S(1)}, f32[2,1,16,128]{3,2,1,0:T(8,128)}, u32[]{:S(2)}) copy-start(f32[2,1,16,128]{3,2,1,0:T(8,128)} %param.10) | copy-start | bytes 49156
  12.5 6.1 %copy-start.7 = (bf16[1,16,128,512]{3,2,1,0:T(8,128)(2,1)S(1)}, bf16[1,16,128,512]{3,2,1,0:T(8,128)(2,1)}, u32[]{:S(2)}) copy-start(bf16[1,16,128,512]{3,2,1,0:T(8,128)(2,1)} %param.9) | copy-start | bytes 6291460
  12.5 58.3 %all-to-all-start.2 = ((bf16[8,8,16384]{2,1,0:T(8,128)(2,1)}), bf16[8,8,16384]{2,1,0:T(8,128)(2,1)}, u32[]{:S(2)}, u32[]{:S(2)}) async-start(bf16[8,8,16384]{2,1,0:T(8,128)(2,1)} %fusion), calls=%async_computation.2 | async-start | bytes 4194304 | tf_op jit(solution)/shard_map/all_to_all | solution.py:266
  20.4 90.6 %collective-permute-start.2 = (bf16[16,128,512]{2,1,0:T(8,128)(2,1)}, bf16[16,128,512]{2,1,0:T(8,128)(2,1)}, u32[]{:S(2)}, u32[]{:S(2)}) collective-permute-start(bf16[16,128,512]{2,1,0:T(8,128)(2,1)} %multiply_convert_fusion.4.own_ref), channel_id=1, source_target_pairs={{0,1},{1,2},{2,3},{4,5},{5,6},{6,7},{8,9},{9,10},{10,11},{12,13},{... | collective-permute-start | bytes 6291464 | tf_op jit(solution)/shard_map/ppermute | solution.py:254
  25.8 85.5 %collective-permute-start.3 = (bf16[16,128,512]{2,1,0:T(8,128)(2,1)}, bf16[16,128,512]{2,1,0:T(8,128)(2,1)}, u32[]{:S(2)}, u32[]{:S(2)}) collective-permute-start(bf16[16,128,512]{2,1,0:T(8,128)(2,1)} %multiply_convert_fusion.4.own_ref), channel_id=1, source_target_pairs={{1,0},{2,1},{3,2},{5,4},{6,5},{7,6},{9,8},{10,9},{11,10},{13,12},{... | collective-permute-start | bytes 6291464 | tf_op jit(solution)/shard_map/ppermute | solution.py:254
  28.8 69.7 %collective-permute-start = (bf16[2,128,512]{2,1,0:T(8,128)(2,1)S(1)}, bf16[2,128,512]{2,1,0:T(8,128)(2,1)S(1)}, u32[]{:S(2)}, u32[]{:S(2)}) collective-permute-start(bf16[2,128,512]{2,1,0:T(8,128)(2,1)S(1)} %get-tuple-element.21), channel_id=1, source_target_pairs={{0,4},{4,8},{8,12},{12,16},{16,20},{20,24},{24,28},{28,0},{1,5},{5... | collective-permute-start | bytes 786440 | tf_op jit(solution)/shard_map/ppermute | solution.py:254
  30.1 79.1 %collective-permute-start.1 = (bf16[2,128,512]{2,1,0:T(8,128)(2,1)S(1)}, bf16[2,128,512]{2,1,0:T(8,128)(2,1)S(1)}, u32[]{:S(2)}, u32[]{:S(2)}) collective-permute-start(bf16[2,128,512]{2,1,0:T(8,128)(2,1)S(1)} %get-tuple-element.20), channel_id=1, source_target_pairs={{0,28},{4,0},{8,4},{12,8},{16,12},{20,16},{24,20},{28,24},{1,29},{... | collective-permute-start | bytes 786440 | tf_op jit(solution)/shard_map/ppermute | solution.py:254
  31.3 113.6 %collective-permute-start.11 = (f32[16,2,128]{2,0,1:T(8,128)S(1)}, f32[16,2,128]{2,0,1:T(8,128)S(1)}, u32[]{:S(2)}, u32[]{:S(2)}) collective-permute-start(f32[16,2,128]{2,0,1:T(8,128)S(1)} %fusion.39), channel_id=1, source_target_pairs={{1,0},{2,1},{3,2},{5,4},{6,5},{7,6},{9,8},{10,9},{11,10},{13,12},{... | collective-permute-start | bytes 49160 | tf_op jit(solution)/shard_map/ppermute | solution.py:254
  33.5 2.5 copy-start.8
  36.0 1.3 copy-start.13
  36.0 1.3 copy-start.12
  36.0 1.3 copy-start.14
  70.9 31.9 %all-to-all-start = ((bf16[8,128,512]{2,1,0:T(8,128)(2,1)}), bf16[8,128,512]{2,1,0:T(8,128)(2,1)S(1)}, u32[]{:S(2)}, u32[]{:S(2)}) async-start(bf16[8,128,512]{2,1,0:T(8,128)(2,1)} %copy.33), calls=%async_computation | async-start | bytes 2097152 | tf_op jit(solution)/shard_map/all_to_all | solution.py:266
  78.3 1.5 copy-start.9
  78.3 1.5 copy-start.10
  98.6 46.3 %collective-permute-start.9 = (f32[16,2,128]{2,0,1:T(8,128)S(1)}, f32[16,2,128]{2,0,1:T(8,128)S(1)}, u32[]{:S(2)}, u32[]{:S(2)}) collective-permute-start(f32[16,2,128]{2,0,1:T(8,128)S(1)} %fusion.39), channel_id=1, source_target_pairs={{0,1},{1,2},{2,3},{4,5},{5,6},{6,7},{8,9},{9,10},{10,11},{12,13},{... | collective-permute-start | bytes 49160 | tf_op jit(solution)/shard_map/ppermute | solution.py:254
  102.7 1.0 copy-start.1
  103.7 27.2 %all-to-all-start.4 = ((f32[8,2,128]{2,1,0:T(2,128)}), f32[8,2,128]{2,1,0:T(2,128)S(1)}, u32[]{:S(2)}, u32[]{:S(2)}) async-start(f32[8,2,128]{2,1,0:T(2,128)} %select_reduce_fusion), calls=%async_computation.4 | async-start | bytes 16384 | tf_op jit(solution)/shard_map/all_to_all | solution.py:266
  109.2 0.7 copy-start.5
  109.9 29.2 %collective-permute-start.7 = (f32[2,2,128]{2,0,1:T(2,128)S(1)}, f32[2,2,128]{2,0,1:T(2,128)S(1)}, u32[]{:S(2)}, u32[]{:S(2)}) collective-permute-start(f32[2,2,128]{2,0,1:T(2,128)S(1)} %get-tuple-element.26), channel_id=1, source_target_pairs={{0,28},{4,0},{8,4},{12,8},{16,12},{20,16},{24,20},{28,24},{1,29},{... | collective-permute-start | bytes 6152 | tf_op jit(solution)/shard_map/ppermute | solution.py:254
  111.1 29.9 %collective-permute-start.5 = (f32[2,2,128]{2,0,1:T(2,128)S(1)}, f32[2,2,128]{2,0,1:T(2,128)S(1)}, u32[]{:S(2)}, u32[]{:S(2)}) collective-permute-start(f32[2,2,128]{2,0,1:T(2,128)S(1)} %get-tuple-element.27), channel_id=1, source_target_pairs={{0,4},{4,8},{8,12},{12,16},{16,20},{20,24},{24,28},{28,0},{1,5},{5... | collective-permute-start | bytes 6152 | tf_op jit(solution)/shard_map/ppermute | solution.py:254
  111.3 1.2 copy-start.2
  112.6 0.9 copy-start.6
  127.9 1.2 copy-start.3
  129.6 15.3 %copy-start.4 = (f32[1280,128]{1,0:T(8,128)S(1)}, f32[1280,128]{1,0:T(8,128)}, u32[]{:S(2)}) copy-start(f32[1280,128]{1,0:T(8,128)} %copy-done.3) | copy-start | bytes 1966084
  130.9 88.8 %all-to-all-start.3 = ((bf16[8,128,512]{2,1,0:T(8,128)(2,1)}), bf16[8,128,512]{2,1,0:T(8,128)(2,1)}, u32[]{:S(2)}, u32[]{:S(2)}) async-start(bf16[8,128,512]{2,1,0:T(8,128)(2,1)} %copy.38), calls=%async_computation.3 | async-start | bytes 2097152 | tf_op jit(solution)/shard_map/all_to_all | solution.py:266
  139.0 82.7 %collective-permute-start.10 = (bf16[16,128,512]{2,1,0:T(8,128)(2,1)S(1)}, bf16[16,128,512]{2,1,0:T(8,128)(2,1)}, u32[]{:S(2)}, u32[]{:S(2)}) collective-permute-start(bf16[16,128,512]{2,1,0:T(8,128)(2,1)S(1)} %get-tuple-element.10), channel_id=1, source_target_pairs={{1,0},{2,1},{3,2},{5,4},{6,5},{7,6},{9,8},{10,9},{11,10},{13,12},{... | collective-permute-start | bytes 6291464 | tf_op jit(solution)/shard_map/ppermute | solution.py:254
  141.0 84.9 %collective-permute-start.8 = (bf16[16,128,512]{2,1,0:T(8,128)(2,1)S(1)}, bf16[16,128,512]{2,1,0:T(8,128)(2,1)}, u32[]{:S(2)}, u32[]{:S(2)}) collective-permute-start(bf16[16,128,512]{2,1,0:T(8,128)(2,1)S(1)} %get-tuple-element.10), channel_id=1, source_target_pairs={{0,1},{1,2},{2,3},{4,5},{5,6},{6,7},{8,9},{9,10},{10,11},{12,13},{... | collective-permute-start | bytes 6291464 | tf_op jit(solution)/shard_map/ppermute | solution.py:254
  205.7 13.4 %collective-permute-start.6 = (bf16[2,128,512]{2,1,0:T(8,128)(2,1)S(1)}, bf16[2,128,512]{2,1,0:T(8,128)(2,1)S(1)}, u32[]{:S(2)}, u32[]{:S(2)}) collective-permute-start(bf16[2,128,512]{2,1,0:T(8,128)(2,1)S(1)} %get-tuple-element.18), channel_id=1, source_target_pairs={{0,28},{4,0},{8,4},{12,8},{16,12},{20,16},{24,20},{28,24},{1,29},{... | collective-permute-start | bytes 786440 | tf_op jit(solution)/shard_map/ppermute | solution.py:254
  205.8 13.7 %collective-permute-start.4 = (bf16[2,128,512]{2,1,0:T(8,128)(2,1)S(1)}, bf16[2,128,512]{2,1,0:T(8,128)(2,1)S(1)}, u32[]{:S(2)}, u32[]{:S(2)}) collective-permute-start(bf16[2,128,512]{2,1,0:T(8,128)(2,1)S(1)} %get-tuple-element.19), channel_id=1, source_target_pairs={{0,4},{4,8},{8,12},{12,16},{16,20},{20,24},{24,28},{28,0},{1,5},{5... | collective-permute-start | bytes 786440 | tf_op jit(solution)/shard_map/ppermute | solution.py:254
  225.9 4.3 %copy-start = (f32[16,128,16]{2,1,0:T(8,128)S(1)}, f32[16,128,16]{2,1,0:T(8,128)}, u32[]{:S(2)}) copy-start(f32[16,128,16]{2,1,0:T(8,128)} %get-tuple-element.41.coef_ref) | copy-start | bytes 393220

commit v3 on v2

--- a/solution.py
+++ b/solution.py
@@ -233,7 +233,8 @@
         in_specs=[pl.BlockSpec(memory_space=pltpu.VMEM)],
         out_specs=(pl.BlockSpec(memory_space=pltpu.VMEM), pl.BlockSpec(memory_space=pltpu.VMEM)),
         scratch_shapes=[pltpu.VMEM((n, n), jnp.float32)],
-        compiler_params=pltpu.CompilerParams(vmem_limit_bytes=32 * 1024 * 1024),
+        compiler_params=pltpu.CompilerParams(vmem_limit_bytes=16 * 1024 * 1024),
+        cost_estimate=pl.CostEstimate(flops=30_000_000_000, bytes_accessed=90_000_000, transcendentals=n),
         name="orthonormalize",
     )(gram_total)
     return upper, growth[0]
@@ -341,6 +342,36 @@
         ),
         name="advance",
     )(tangents, before, own, after, above, below, far, weights, far_weights, coef)
+
+
+def place_kernel(target_ref, got_ref, out_ref):
+    sources, capacity, size, _ = got_ref.shape
+    out_ref[...] = jnp.zeros_like(out_ref)
+    for s in range(sources):
+
+        def add(c, carry):
+            at = target_ref[s, c]
+            lanes = slice(s * size, (s + 1) * size)
+            held = out_ref[at, :, lanes].astype(jnp.float32)
+            out_ref[at, :, lanes] = (held + got_ref[s, c].astype(jnp.float32)).astype(jnp.bfloat16)
+            return carry
+
+        lax.fori_loop(0, capacity, add, 0)
+
+
+def placed(got_weights, got_target, blocks):
+    sources, _, size, _ = got_weights.shape
+    return pl.pallas_call(
+        place_kernel,
+        out_shape=jax.ShapeDtypeStruct((blocks, size, sources * size), jnp.bfloat16),
+        in_specs=[
+            pl.BlockSpec(memory_space=pltpu.SMEM),
+            pl.BlockSpec(memory_space=pltpu.VMEM),
+        ],
+        out_specs=pl.BlockSpec(memory_space=pltpu.VMEM),
+        compiler_params=pltpu.CompilerParams(vmem_limit_bytes=32 * 1024 * 1024),
+        name="place_pairs",
+    )(got_target, got_weights)
 
 
 def body(
@@ -398,26 +429,21 @@
     scaled = (state * slope[0][..., None]).astype(jnp.bfloat16)
     edges = neighbours(scaled)
     far = exchanged(bundle(scaled))
-    got_weights = exchanged(slot_weights.reshape(col_count, capacity, size * size))
-    got_target = exchanged(slot_target.astype(jnp.int32).reshape(col_count, 1, capacity))
-    bundle_slope = jnp.sum(jnp.where(bundle_pick[:, :, None, None], slope.transpose(1, 0, 2)[None], 0.0), axis=1)
-    far_slope = exchanged(bundle_slope)
+    got_weights = exchanged(slot_weights.reshape(col_count, capacity, size, size))
+    bundle_slope = jnp.sum(
+        jnp.where(bundle_pick[:, :, None, None], slope.transpose(1, 0, 2)[None], 0.0), axis=1
+    )
+    target_row = jnp.pad(
+        slot_target.astype(jnp.float32).reshape(col_count, 1, capacity),
+        ((0, 0), (0, 0), (0, size - capacity)),
+    )
+    far_notes = exchanged(jnp.concatenate([bundle_slope, target_row], axis=1))
+    far_slope = far_notes[:, :steps]
+    got_target = far_notes[:, steps, :capacity].astype(jnp.int32)
     edge_slope = [
         edge.transpose(1, 0, 2) for edge in neighbours(slope.transpose(1, 0, 2))
     ]
-    hit = (
-        got_target.reshape(col_count, 1, capacity)
-        == jnp.arange(blocks, dtype=jnp.int32)[None, :, None]
-    ).astype(jnp.bfloat16)
-    far_weights = (
-        lax.dot_general(
-            hit, got_weights, (((2,), (1,)), ((0,), (0,))), preferred_element_type=jnp.float32
-        )
-        .astype(jnp.bfloat16)
-        .reshape(col_count, blocks, size, size)
-        .transpose(1, 2, 0, 3)
-        .reshape(blocks, size, col_count * size)
-    )
+    far_weights = placed(got_weights, got_target, blocks)
 
     reversal = jnp.where(block_label == 1, INHIBIT_REVERSAL, EXCITE_REVERSAL).astype(jnp.float32)
     edge_row = jnp.full((1, reversal.shape[1]), EXCITE_REVERSAL, jnp.float32)
@@ -447,6 +473,7 @@
         gram = summed(gram)
         last = t == steps - 1
         if not last:
+            gram, advanced = lax.optimization_barrier((gram, advanced))
             edges = neighbours(advanced)
             far = exchanged(bundle(advanced))
         upper, grown = orthonormalize(gram, neurons, vectors)

time: 297 us -> 278 us (0.936)
  local copies, waits for them, and re-layouts: 30.7 us -> 17.6 us
  starting transfers between devices: 54.2 us -> 47.7 us
  waiting for transfers between devices: 40.2 us -> 46.4 us
  Pallas kernels: 138 us -> 132 us
  other arithmetic: 7.76 us -> 12.7 us
  matrix products: 24.4 us -> 20.1 us
    ppermute x12, waiting for transfers between devices: 8.68 us -> 25.7 us  [shifted(): return lax.ppermute(value, axis, pairs)]
    reshape x3 -> x0, local copies, waits for them, and re-layouts: 13.6 us -> none  [the longest x2 12.9 us: body(): far_weights = lax.dot_general(hit, got_weights, (((2,), (1,)), ((0,), (0,...]
    all_to_all x5 -> x4, waiting for transfers between devices: 31.5 us -> 20.7 us  [exchanged(): return lax.all_to_all(value, 'col', split_axis=0, concat_axis=0, tiled=True)]
    all_to_all x5 -> x4, starting transfers between devices: 29.6 us -> 21.3 us  [exchanged(): return lax.all_to_all(value, 'col', split_axis=0, concat_axis=0, tiled=True)]
    pallas_call x2, Pallas kernels: 65.3 us -> 57.3 us  [summed(): pl.pallas_call(functools.partial(sum_kernel, groups, per_col), out_shape=...]
    unnamed x34 -> x22, local copies, waits for them, and re-layouts: 10 us -> 10.4 us
  transfers between devices with their start and end apart: 17 -> 16, of which waited for: 2 -> 5; matrix products, arithmetic and copies ran while one was open for 16% -> 12% of each run, Pallas kernels for 25% -> 9%
where the time goes in v3:
time: 278 us
  Pallas kernels  132 us (47%)
  starting transfers between devices  47.7 us (17%)
  waiting for transfers between devices  46.4 us (17%)
  matrix products  20.1 us (7%)
  local copies, waits for them, and re-layouts  17.6 us (6%)
  other arithmetic  12.7 us (5%)
    pallas_call x2, Pallas kernels, summed(): pl.pallas_call(functools.partial(sum_kernel, groups, per_col), out_shape=...  57.3 us
    pallas_call x2, Pallas kernels, orthonormalize(): pl.pallas_call(functools.partial(orthonormal_kernel, count), out_shape=(j...  43.8 us
    pallas_call x2, Pallas kernels, advance(): pl.pallas_call(functools.partial(advance_kernel, per_step), grid=(blocks...  29.1 us
    ppermute x12, starting transfers between devices, shifted(): return lax.ppermute(value, axis, pairs)  26.3 us
    ppermute x12, waiting for transfers between devices, shifted(): return lax.ppermute(value, axis, pairs)  25.7 us
    all_to_all x4, starting transfers between devices, exchanged(): return lax.all_to_all(value, 'col', split_axis=0, concat_axis=0, tiled=True)  21.3 us
    all_to_all x4, waiting for transfers between devices, exchanged(): return lax.all_to_all(value, 'col', split_axis=0, concat_axis=0, tiled=True)  20.7 us
    dot_general x7, matrix products, rotated(): jnp.dot(cells, upper, preferred_element_type=jnp.float32)  16.9 us
  transfers between devices with their start and end apart: 16, of which 5 were waited for; matrix products, arithmetic and copies ran while one was open for 12% of the time, Pallas kernels for 9%

profile of v3, /device:TPU:25, one launch (start us, length us, event | category | flops | bytes accessed | tf_op | source)
XLA Modules:
  0.0 277.6 jit_solution(2936968762593983152)
XLA Ops:
  5.2 5.5 %all-to-all-start.1 = ((f32[8,3,128]{2,1,0:T(4,128)}), f32[8,3,128]{2,1,0:T(4,128)S(1)}, u32[]{:S(2)}, u32[]{:S(2)}) async-start(f32[8,3,128]{2,1,0:T(4,128)} %select_maximum_fusion), calls=%async_computation.1 | async-start | bytes 32768 | tf_op jit(solution)/shard_map/all_to_all | solution.py:267
  10.7 2.1 fusion
  12.8 1.9 copy.49
  14.8 5.6 %all-to-all-start.2 = ((bf16[8,8,128,128]{3,2,1,0:T(8,128)(2,1)}), bf16[8,8,128,128]{3,2,1,0:T(8,128)(2,1)S(1)}, u32[]{:S(2)}, u32[]{:S(2)}) async-start(bf16[8,8,128,128]{3,2,1,0:T(8,128)(2,1)} %copy.49), calls=%async_computation.2 | async-start | bytes 4194304 | tf_op jit(solution)/shard_map/all_to_all | solution.py:267
  20.4 3.5 %multiply_convert_fusion.4.own_ref = bf16[16,128,512]{2,1,0:T(8,128)(2,1)} fusion(f32[16,128]{1,0:T(8,128)S(1)} %get-tuple-element.33, bf16[1,16,128,512]{3,2,1,0:T(8,128)(2,1)} %param.9), kind=kLoop, calls=%fused_computation.7 | loop fusion | flops 3145728 | bytes 4202496 | tf_op jit(solution)/shard_map/convert_element_type | solution.py:429
  23.9 4.9 %collective-permute-start.2 = (bf16[16,128,512]{2,1,0:T(8,128)(2,1)}, bf16[16,128,512]{2,1,0:T(8,128)(2,1)}, u32[]{:S(2)}, u32[]{:S(2)}) collective-permute-start(bf16[16,128,512]{2,1,0:T(8,128)(2,1)} %multiply_convert_fusion.4.own_ref), channel_id=1, source_target_pairs={{0,1},{1,2},{2,3},{4,5},{5,6},{6,7},{8,9},{9,10},{10,11},{12,13},{... | collective-permute-start | bytes 6291464 | tf_op jit(solution)/shard_map/ppermute | solution.py:255
  28.8 1.9 collective-permute-start.3
  30.7 3.6 %collective-permute-start.9 = (f32[16,2,128]{2,0,1:T(8,128)S(1)}, f32[16,2,128]{2,0,1:T(8,128)S(1)}, u32[]{:S(2)}, u32[]{:S(2)}) collective-permute-start(f32[16,2,128]{2,0,1:T(8,128)S(1)} %fusion.37), channel_id=1, source_target_pairs={{0,1},{1,2},{2,3},{4,5},{5,6},{6,7},{8,9},{9,10},{10,11},{12,13},{... | collective-permute-start | bytes 49160 | tf_op jit(solution)/shard_map/ppermute | solution.py:255
  34.4 1.9 collective-permute-start.11
  39.2 2.4 copy.40
  46.7 20.6 %all-to-all-done.2.got_ref = bf16[8,8,128,128]{3,2,1,0:T(8,128)(2,1)S(1)} async-done(((bf16[8,8,128,128]{3,2,1,0:T(8,128)(2,1)}), bf16[8,8,128,128]{3,2,1,0:T(8,128)(2,1)S(1)}, u32[]{:S(2)}, u32[]{:S(2)}) %all-to-all-start.2) | async-done | bytes 2097184 | tf_op jit(solution)/shard_map/all_to_all | solution.py:267
  67.4 5.0 %all-to-all-start = ((bf16[8,128,512]{2,1,0:T(8,128)(2,1)}), bf16[8,128,512]{2,1,0:T(8,128)(2,1)}, u32[]{:S(2)}, u32[]{:S(2)}) async-start(bf16[8,128,512]{2,1,0:T(8,128)(2,1)} %copy.31), calls=%async_computation | async-start | bytes 2097152 | tf_op jit(solution)/shard_map/all_to_all | solution.py:267
  73.0 3.3 %maximum_maximum_fusion.1 = (f32[16,128,16]{2,1,0:T(8,128)}, f32[16,128,16]{2,1,0:T(8,128)S(1)}) fusion(f32[16,128,1]{2,1,0:T(8,128)} %copy.37, f32[16,128,8]{2,1,0:T(8,128)S(1)} %get-tuple-element.34, f32[16]{0:T(128)S(1)} %pad.10.clone, f32[16,128,1]{2,1,0:T(8,128)} %copy.35, f32[16,128,8]{2,1,0:T(8,128)S(1)} %get-tuple-element.35), kind=kLoop, calls=%fused_computation.25 | loop fusion | flops 131072 | bytes 409664 | tf_op jit(solution)/shard_map/concatenate | solution.py:461
  78.6 9.9 %collective-permute-done.7 = f32[2,2,128]{2,0,1:T(2,128)S(1)} collective-permute-done((f32[2,2,128]{2,0,1:T(2,128)S(1)}, f32[2,2,128]{2,0,1:T(2,128)S(1)}, u32[]{:S(2)}, u32[]{:S(2)}) %collective-permute-start.7) | collective-permute-done | bytes 2080 | tf_op jit(solution)/shard_map/ppermute | solution.py:255
  92.0 2.0 place_pairs.1.far_weights_ref
  94.0 2.0 copy-done
  96.0 7.0 %collective-permute-done.before_ref = bf16[2,128,512]{2,1,0:T(8,128)(2,1)S(1)} collective-permute-done((bf16[2,128,512]{2,1,0:T(8,128)(2,1)S(1)}, bf16[2,128,512]{2,1,0:T(8,128)(2,1)S(1)}, u32[]{:S(2)}, u32[]{:S(2)}) %collective-permute-start) | collective-permute-done | bytes 262176 | tf_op jit(solution)/shard_map/ppermute | solution.py:255
  104.6 14.7 %advance.2 = (bf16[16,128,512]{2,1,0:T(8,128)(2,1)S(1)}, f32[1280,128]{1,0:T(8,128)S(1)}) custom-call(bf16[16,128,512]{2,1,0:T(8,128)(2,1)} %bitcast.110, bf16[2,128,512]{2,1,0:T(8,128)(2,1)S(1)} %collective-permute-done.before_ref, bf16[16,128,512]{2,1,0:T(8,128)(2,1)} %multiply_convert_fusion.4.own_ref, bf16[2,128,512]{2,1,0:T(8,128)(2,1)S(1)} %copy-done.3, ...), custom_call_target="tpu_custom_call" | custom-call | tf_op jit(solution)/shard_map/advance/pallas_call | solution.py:321
  119.3 31.9 %sum_gram.2.packed_ref = f32[1280,128]{1,0:T(8,128)S(1)} custom-call(f32[1280,128]{1,0:T(8,128)S(1)} %get-tuple-element.12.packed_ref), custom_call_target="tpu_custom_call" | custom-call | tf_op jit(solution)/shard_map/sum_gram/pallas_call | solution.py:134
  151.3 2.7 collective-permute-start.8
  154.0 3.0 %collective-permute-start.10 = (bf16[16,128,512]{2,1,0:T(8,128)(2,1)S(1)}, bf16[16,128,512]{2,1,0:T(8,128)(2,1)}, u32[]{:S(2)}, u32[]{:S(2)}) collective-permute-start(bf16[16,128,512]{2,1,0:T(8,128)(2,1)S(1)} %get-tuple-element.14), channel_id=1, source_target_pairs={{1,0},{2,1},{3,2},{5,4},{6,5},{7,6},{9,8},{10,9},{11,10},{13,12},{... | collective-permute-start | bytes 6291464 | tf_op jit(solution)/shard_map/ppermute | solution.py:255
  160.0 5.3 %all-to-all-start.3 = ((bf16[8,128,512]{2,1,0:T(8,128)(2,1)}), bf16[8,128,512]{2,1,0:T(8,128)(2,1)}, u32[]{:S(2)}, u32[]{:S(2)}) async-start(bf16[8,128,512]{2,1,0:T(8,128)(2,1)} %copy.36), calls=%async_computation.3 | async-start | bytes 2097152 | tf_op jit(solution)/shard_map/all_to_all | solution.py:267
  165.2 21.9 %orthonormalize.2 = (bf16[512,512]{1,0:T(8,128)(2,1)S(1)}, f32[1,512]{1,0:T(1,128)S(1)}) custom-call(f32[1280,128]{1,0:T(8,128)S(1)} %sum_gram.2.packed_ref), custom_call_target="tpu_custom_call" | custom-call | flops 30000001024 | bytes 90000000 | tf_op jit(solution)/shard_map/orthonormalize/pallas_call | solution.py:227
  189.6 3.3 %multiply_convert_fusion.2 = (bf16[16,128,512]{2,1,0:T(8,128)(2,1)}, bf16[16,128,512]{2,1,0:T(8,128)(2,1)}) fusion(f32[16,128]{1,0:T(8,128)S(1)} %get-tuple-element.32, bf16[16,128,512]{2,1,0:T(8,128)(2,1)S(1)} %get-tuple-element.14, bf16[512,512]{1,0:T(8,128)(2,1)S(1)} %get-tuple-element.16), kind=kOutput, calls=%fused_computation.5 | convolution fusion | flops 1077936128 | bytes 6823936 | tf_op jit(solution)/shard_map/dot_general | solution.py:483
  192.9 7.0 %collective-permute-done.4 = bf16[2,128,512]{2,1,0:T(8,128)(2,1)S(1)} collective-permute-done((bf16[2,128,512]{2,1,0:T(8,128)(2,1)S(1)}, bf16[2,128,512]{2,1,0:T(8,128)(2,1)S(1)}, u32[]{:S(2)}, u32[]{:S(2)}) %collective-permute-start.4) | collective-permute-done | bytes 262176 | tf_op jit(solution)/shard_map/ppermute | solution.py:255
  202.3 1.9 multiply_convert_fusion.6
  204.3 4.2 %multiply_convert_fusion.1.above_ref = bf16[16,128,512]{2,1,0:T(8,128)(2,1)} fusion(f32[16,128]{1,0:T(8,128)S(1)} %slice_bitcast_fusion.1, bf16[16,128,512]{2,1,0:T(8,128)(2,1)} %collective-permute-done.8, bf16[512,512]{1,0:T(8,128)(2,1)S(1)} %get-tuple-element.16), kind=kOutput, calls=%fused_computation.4 | convolution fusion | flops 1077936128 | bytes 4726784 | tf_op jit(solution)/shard_map/dot_general | solution.py:483
  208.5 4.3 %multiply_convert_fusion.below_ref = bf16[16,128,512]{2,1,0:T(8,128)(2,1)} fusion(f32[16,128]{1,0:T(8,128)S(1)} %slice_bitcast_fusion, bf16[16,128,512]{2,1,0:T(8,128)(2,1)} %collective-permute-done.10, bf16[512,512]{1,0:T(8,128)(2,1)S(1)} %get-tuple-element.16), kind=kOutput, calls=%fused_computation.3 | convolution fusion | flops 1077936128 | bytes 4726784 | tf_op jit(solution)/shard_map/dot_general | solution.py:483
  212.8 14.4 %advance.3 = (bf16[16,128,512]{2,1,0:T(8,128)(2,1)S(1)}, f32[1280,128]{1,0:T(8,128)S(1)}) custom-call(bf16[16,128,512]{2,1,0:T(8,128)(2,1)} %get-tuple-element.48.tangents_ref, bf16[2,128,512]{2,1,0:T(8,128)(2,1)S(1)} %fusion.6.before_ref, bf16[16,128,512]{2,1,0:T(8,128)(2,1)} %get-tuple-element.47.own_ref, bf16[2,128,512]{2,1,0:T(8,128)(2,1)S(1)} %fusion.3.after_ref, ...), custom_call_target="tpu_custom_call" | custom-call | tf_op jit(solution)/shard_map/advance/pallas_call | solution.py:321
  227.2 25.3 %sum_gram.3.packed_ref = f32[1280,128]{1,0:T(8,128)S(1)} custom-call(f32[1280,128]{1,0:T(8,128)S(1)} %get-tuple-element.18.packed_ref), custom_call_target="tpu_custom_call" | custom-call | tf_op jit(solution)/shard_map/sum_gram/pallas_call | solution.py:134
  252.6 21.9 %orthonormalize.3 = (bf16[512,512]{1,0:T(8,128)(2,1)S(1)}, f32[1,512]{1,0:T(1,128)S(1)}) custom-call(f32[1280,128]{1,0:T(8,128)S(1)} %sum_gram.3.packed_ref), custom_call_target="tpu_custom_call" | custom-call | flops 30000001024 | bytes 90000000 | tf_op jit(solution)/shard_map/orthonormalize/pallas_call | solution.py:227
  274.5 2.6 convert_bitcast_fusion
  (82 shorter events, 29.0 us)
Async XLA Ops:
  5.2 9.5 %all-to-all-start.1 = ((f32[8,3,128]{2,1,0:T(4,128)}), f32[8,3,128]{2,1,0:T(4,128)S(1)}, u32[]{:S(2)}, u32[]{:S(2)}) async-start(f32[8,3,128]{2,1,0:T(4,128)} %select_maximum_fusion), calls=%async_computation.1 | async-start | bytes 32768 | tf_op jit(solution)/shard_map/all_to_all | solution.py:267
  14.8 5.6 %copy-start.5 = (f32[2,1,16,128]{3,2,1,0:T(8,128)S(1)}, f32[2,1,16,128]{3,2,1,0:T(8,128)}, u32[]{:S(2)}) copy-start(f32[2,1,16,128]{3,2,1,0:T(8,128)} %param.10) | copy-start | bytes 49156
  14.8 52.6 %all-to-all-start.2 = ((bf16[8,8,128,128]{3,2,1,0:T(8,128)(2,1)}), bf16[8,8,128,128]{3,2,1,0:T(8,128)(2,1)S(1)}, u32[]{:S(2)}, u32[]{:S(2)}) async-start(bf16[8,8,128,128]{3,2,1,0:T(8,128)(2,1)} %copy.49), calls=%async_computation.2 | async-start | bytes 4194304 | tf_op jit(solution)/shard_map/all_to_all | solution.py:267
  20.4 17.2 %copy-start.4 = (bf16[1,16,128,512]{3,2,1,0:T(8,128)(2,1)S(1)}, bf16[1,16,128,512]{3,2,1,0:T(8,128)(2,1)}, u32[]{:S(2)}) copy-start(bf16[1,16,128,512]{3,2,1,0:T(8,128)(2,1)} %param.9) | copy-start | bytes 6291460
  23.9 79.7 %collective-permute-start.2 = (bf16[16,128,512]{2,1,0:T(8,128)(2,1)}, bf16[16,128,512]{2,1,0:T(8,128)(2,1)}, u32[]{:S(2)}, u32[]{:S(2)}) collective-permute-start(bf16[16,128,512]{2,1,0:T(8,128)(2,1)} %multiply_convert_fusion.4.own_ref), channel_id=1, source_target_pairs={{0,1},{1,2},{2,3},{4,5},{5,6},{6,7},{8,9},{9,10},{10,11},{12,13},{... | collective-permute-start | bytes 6291464 | tf_op jit(solution)/shard_map/ppermute | solution.py:255
  28.8 74.9 %collective-permute-start.3 = (bf16[16,128,512]{2,1,0:T(8,128)(2,1)}, bf16[16,128,512]{2,1,0:T(8,128)(2,1)}, u32[]{:S(2)}, u32[]{:S(2)}) collective-permute-start(bf16[16,128,512]{2,1,0:T(8,128)(2,1)} %multiply_convert_fusion.4.own_ref), channel_id=1, source_target_pairs={{1,0},{2,1},{3,2},{5,4},{6,5},{7,6},{9,8},{10,9},{11,10},{13,12},{... | collective-permute-start | bytes 6291464 | tf_op jit(solution)/shard_map/ppermute | solution.py:255
  30.7 59.3 %collective-permute-start.9 = (f32[16,2,128]{2,0,1:T(8,128)S(1)}, f32[16,2,128]{2,0,1:T(8,128)S(1)}, u32[]{:S(2)}, u32[]{:S(2)}) collective-permute-start(f32[16,2,128]{2,0,1:T(8,128)S(1)} %fusion.37), channel_id=1, source_target_pairs={{0,1},{1,2},{2,3},{4,5},{5,6},{6,7},{8,9},{9,10},{10,11},{12,13},{... | collective-permute-start | bytes 49160 | tf_op jit(solution)/shard_map/ppermute | solution.py:255
  34.4 57.6 %collective-permute-start.11 = (f32[16,2,128]{2,0,1:T(8,128)S(1)}, f32[16,2,128]{2,0,1:T(8,128)S(1)}, u32[]{:S(2)}, u32[]{:S(2)}) collective-permute-start(f32[16,2,128]{2,0,1:T(8,128)S(1)} %fusion.37), channel_id=1, source_target_pairs={{1,0},{2,1},{3,2},{5,4},{6,5},{7,6},{9,8},{10,9},{11,10},{13,12},{... | collective-permute-start | bytes 49160 | tf_op jit(solution)/shard_map/ppermute | solution.py:255
  36.3 41.1 %collective-permute-start.5 = (f32[2,2,128]{2,0,1:T(2,128)S(1)}, f32[2,2,128]{2,0,1:T(2,128)S(1)}, u32[]{:S(2)}, u32[]{:S(2)}) collective-permute-start(f32[2,2,128]{2,0,1:T(2,128)S(1)} %get-tuple-element.31), channel_id=1, source_target_pairs={{0,4},{4,8},{8,12},{12,16},{16,20},{20,24},{24,28},{28,0},{1,5},{5... | collective-permute-start | bytes 6152 | tf_op jit(solution)/shard_map/ppermute | solution.py:255
  39.1 2.5 copy-start.8
  42.2 1.3 copy-start.6
  42.2 2.7 copy-start.7
  67.4 36.3 %all-to-all-start = ((bf16[8,128,512]{2,1,0:T(8,128)(2,1)}), bf16[8,128,512]{2,1,0:T(8,128)(2,1)}, u32[]{:S(2)}, u32[]{:S(2)}) async-start(bf16[8,128,512]{2,1,0:T(8,128)(2,1)} %copy.31), calls=%async_computation | async-start | bytes 2097152 | tf_op jit(solution)/shard_map/all_to_all | solution.py:267
  77.4 11.1 %collective-permute-start.7 = (f32[2,2,128]{2,0,1:T(2,128)S(1)}, f32[2,2,128]{2,0,1:T(2,128)S(1)}, u32[]{:S(2)}, u32[]{:S(2)}) collective-permute-start(f32[2,2,128]{2,0,1:T(2,128)S(1)} %get-tuple-element.30), channel_id=1, source_target_pairs={{0,28},{4,0},{8,4},{12,8},{16,12},{20,16},{24,20},{28,24},{1,29},{... | collective-permute-start | bytes 6152 | tf_op jit(solution)/shard_map/ppermute | solution.py:255
  88.6 14.4 %collective-permute-start = (bf16[2,128,512]{2,1,0:T(8,128)(2,1)S(1)}, bf16[2,128,512]{2,1,0:T(8,128)(2,1)S(1)}, u32[]{:S(2)}, u32[]{:S(2)}) collective-permute-start(bf16[2,128,512]{2,1,0:T(8,128)(2,1)S(1)} %get-tuple-element.25), channel_id=1, source_target_pairs={{0,4},{4,8},{8,12},{12,16},{16,20},{20,24},{24,28},{28,0},{1,5},{5... | collective-permute-start | bytes 786440 | tf_op jit(solution)/shard_map/ppermute | solution.py:255
  90.1 12.9 %collective-permute-start.1 = (bf16[2,128,512]{2,1,0:T(8,128)(2,1)S(1)}, bf16[2,128,512]{2,1,0:T(8,128)(2,1)S(1)}, u32[]{:S(2)}, u32[]{:S(2)}) collective-permute-start(bf16[2,128,512]{2,1,0:T(8,128)(2,1)S(1)} %get-tuple-element.24), channel_id=1, source_target_pairs={{0,28},{4,0},{8,4},{12,8},{16,12},{20,16},{24,20},{28,24},{1,29},{... | collective-permute-start | bytes 786440 | tf_op jit(solution)/shard_map/ppermute | solution.py:255
  94.0 2.0 copy-start
  103.0 0.7 copy-start.2
  103.7 1.0 copy-start.3
  151.3 53.0 %collective-permute-start.8 = (bf16[16,128,512]{2,1,0:T(8,128)(2,1)S(1)}, bf16[16,128,512]{2,1,0:T(8,128)(2,1)}, u32[]{:S(2)}, u32[]{:S(2)}) collective-permute-start(bf16[16,128,512]{2,1,0:T(8,128)(2,1)S(1)} %get-tuple-element.14), channel_id=1, source_target_pairs={{0,1},{1,2},{2,3},{4,5},{5,6},{6,7},{8,9},{9,10},{10,11},{12,13},{... | collective-permute-start | bytes 6291464 | tf_op jit(solution)/shard_map/ppermute | solution.py:255
  154.0 54.5 %collective-permute-start.10 = (bf16[16,128,512]{2,1,0:T(8,128)(2,1)S(1)}, bf16[16,128,512]{2,1,0:T(8,128)(2,1)}, u32[]{:S(2)}, u32[]{:S(2)}) collective-permute-start(bf16[16,128,512]{2,1,0:T(8,128)(2,1)S(1)} %get-tuple-element.14), channel_id=1, source_target_pairs={{1,0},{2,1},{3,2},{5,4},{6,5},{7,6},{9,8},{10,9},{11,10},{13,12},{... | collective-permute-start | bytes 6291464 | tf_op jit(solution)/shard_map/ppermute | solution.py:255
  160.0 42.4 %all-to-all-start.3 = ((bf16[8,128,512]{2,1,0:T(8,128)(2,1)}), bf16[8,128,512]{2,1,0:T(8,128)(2,1)}, u32[]{:S(2)}, u32[]{:S(2)}) async-start(bf16[8,128,512]{2,1,0:T(8,128)(2,1)} %copy.36), calls=%async_computation.3 | async-start | bytes 2097152 | tf_op jit(solution)/shard_map/all_to_all | solution.py:267
  187.2 12.6 %collective-permute-start.4 = (bf16[2,128,512]{2,1,0:T(8,128)(2,1)S(1)}, bf16[2,128,512]{2,1,0:T(8,128)(2,1)S(1)}, u32[]{:S(2)}, u32[]{:S(2)}) collective-permute-start(bf16[2,128,512]{2,1,0:T(8,128)(2,1)S(1)} %get-tuple-element.23), channel_id=1, source_target_pairs={{0,4},{4,8},{8,12},{12,16},{16,20},{20,24},{24,28},{28,0},{1,5},{5... | collective-permute-start | bytes 786440 | tf_op jit(solution)/shard_map/ppermute | solution.py:255
  188.4 13.6 %collective-permute-start.6 = (bf16[2,128,512]{2,1,0:T(8,128)(2,1)S(1)}, bf16[2,128,512]{2,1,0:T(8,128)(2,1)S(1)}, u32[]{:S(2)}, u32[]{:S(2)}) collective-permute-start(bf16[2,128,512]{2,1,0:T(8,128)(2,1)S(1)} %get-tuple-element.22), channel_id=1, source_target_pairs={{0,28},{4,0},{8,4},{12,8},{16,12},{20,16},{24,20},{28,24},{1,29},{... | collective-permute-start | bytes 786440 | tf_op jit(solution)/shard_map/ppermute | solution.py:255
  208.5 4.3 %copy-start.1 = (f32[16,128,16]{2,1,0:T(8,128)S(1)}, f32[16,128,16]{2,1,0:T(8,128)}, u32[]{:S(2)}) copy-start(f32[16,128,16]{2,1,0:T(8,128)} %get-tuple-element.45.coef_ref) | copy-start | bytes 393220

commit v4 on v3

--- a/solution.py
+++ b/solution.py
@@ -145,6 +145,7 @@
         compiler_params=pltpu.CompilerParams(
             collective_id=0, has_side_effects=True, vmem_limit_bytes=16 * 1024 * 1024
         ),
+        cost_estimate=pl.CostEstimate(flops=0, bytes_accessed=80_000_000, transcendentals=0),
         name="sum_gram",
     )(packed)
 
@@ -255,12 +256,12 @@
     return lax.ppermute(value, axis, pairs)
 
 
-def neighbours(cells):
-    before = shifted(cells[-2:], "col", 1, True)
-    after = shifted(cells[:2], "col", -1, True)
-    above = shifted(cells, "layer", 1, False)
-    below = shifted(cells, "layer", -1, False)
-    return before, after, above, below
+def column_edges(cells):
+    return shifted(cells[-2:], "col", 1, True), shifted(cells[:2], "col", -1, True)
+
+
+def layer_edges(cells):
+    return shifted(cells, "layer", 1, False), shifted(cells, "layer", -1, False)
 
 
 def exchanged(value):
@@ -342,6 +343,72 @@
         ),
         name="advance",
     )(tangents, before, own, after, above, below, far, weights, far_weights, coef)
+
+
+def exchange_kernel(parts, *refs):
+    given, got, sems = refs[:parts], refs[parts : 2 * parts], refs[2 * parts]
+    count = given[0].shape[0]
+    me, layer = lax.axis_index("col"), lax.axis_index("layer")
+    barrier = pltpu.get_barrier_semaphore()
+
+    def peer(step):
+        k = lax.rem(me + step, count)
+        return k, {"col": k, "layer": layer}
+
+    def remote(part, k, slot, device):
+        return pltpu.make_async_remote_copy(
+            src_ref=given[part].at[k],
+            dst_ref=got[part].at[slot],
+            send_sem=sems.at[2 * part, k],
+            recv_sem=sems.at[2 * part + 1, slot],
+            device_id=device,
+            device_id_type=MESH,
+        )
+
+    def greet(step, carry):
+        _, device = peer(step)
+        pl.semaphore_signal(barrier, inc=1, device_id=device, device_id_type=MESH)
+        return carry
+
+    def send(step, carry):
+        k, device = peer(step)
+        for part in range(parts):
+            remote(part, k, me, device).start()
+        return carry
+
+    def receive(step, carry):
+        k, device = peer(step)
+        for part in range(parts):
+            copy = remote(part, k, k, device)
+            copy.wait_send()
+            copy.wait_recv()
+        return carry
+
+    lax.fori_loop(1, count, greet, 0)
+    pl.semaphore_wait(barrier, count - 1)
+    lax.fori_loop(1, count, send, 0)
+    for part in range(parts):
+        got[part][me] = given[part][me]
+    lax.fori_loop(1, count, receive, 0)
+
+
+def exchanged_together(*values):
+    parts = len(values)
+    vmem = pl.BlockSpec(memory_space=pltpu.VMEM)
+    return pl.pallas_call(
+        functools.partial(exchange_kernel, parts),
+        out_shape=tuple(jax.ShapeDtypeStruct(v.shape, v.dtype) for v in values),
+        in_specs=[vmem] * parts,
+        out_specs=(vmem,) * parts,
+        scratch_shapes=[pltpu.SemaphoreType.DMA((2 * parts, values[0].shape[0]))],
+        compiler_params=pltpu.CompilerParams(
+            collective_id=1, has_side_effects=True, vmem_limit_bytes=24 * 1024 * 1024
+        ),
+        cost_estimate=pl.CostEstimate(
+            flops=0, bytes_accessed=200_000_000, transcendentals=0
+        ),
+        name="exchange",
+    )(*values)
 
 
 def place_kernel(target_ref, got_ref, out_ref):
@@ -427,9 +494,12 @@
     slope = gain_slope(volt)
     state = tangents[0]
     scaled = (state * slope[0][..., None]).astype(jnp.bfloat16)
-    edges = neighbours(scaled)
-    far = exchanged(bundle(scaled))
-    got_weights = exchanged(slot_weights.reshape(col_count, capacity, size, size))
+    slope_rows = slope.transpose(1, 0, 2)
+    edge_slope = [
+        edge.transpose(1, 0, 2) for edge in column_edges(slope_rows) + layer_edges(slope_rows)
+    ]
+    beside = column_edges(scaled)
+    over = layer_edges(scaled)
     bundle_slope = jnp.sum(
         jnp.where(bundle_pick[:, :, None, None], slope.transpose(1, 0, 2)[None], 0.0), axis=1
     )
@@ -437,12 +507,13 @@
         slot_target.astype(jnp.float32).reshape(col_count, 1, capacity),
         ((0, 0), (0, 0), (0, size - capacity)),
     )
-    far_notes = exchanged(jnp.concatenate([bundle_slope, target_row], axis=1))
+    notes = jnp.concatenate([bundle_slope, target_row], axis=1)
+    notes = jnp.pad(notes, ((0, 0), (0, -notes.shape[1] % 8), (0, 0)))
+    sent = (slot_weights.reshape(col_count, capacity, size, size), bundle(scaled), notes)
+    sent, beside = lax.optimization_barrier((sent, beside))
+    got_weights, far, far_notes = exchanged_together(*sent)
     far_slope = far_notes[:, :steps]
     got_target = far_notes[:, steps, :capacity].astype(jnp.int32)
-    edge_slope = [
-        edge.transpose(1, 0, 2) for edge in neighbours(slope.transpose(1, 0, 2))
-    ]
     far_weights = placed(got_weights, got_target, blocks)
 
     reversal = jnp.where(block_label == 1, INHIBIT_REVERSAL, EXCITE_REVERSAL).astype(jnp.float32)
@@ -467,14 +538,18 @@
             axis=-1,
         )
         advanced, gram = advance(
-            state, edges[0], scaled, edges[1], edges[2], edges[3],
+            state, beside[0], scaled, beside[1], over[0], over[1],
             far.reshape(col_count * size, vectors), local_weights[0], far_weights, coef,
         )
-        gram = summed(gram)
         last = t == steps - 1
         if not last:
-            gram, advanced = lax.optimization_barrier((gram, advanced))
-            edges = neighbours(advanced)
+            beside = column_edges(advanced)
+        gram = summed(gram)
+        if not last:
+            gram, advanced, beside, edge_slope = lax.optimization_barrier(
+                (gram, advanced, beside, edge_slope)
+            )
+            over = layer_edges(advanced)
             far = exchanged(bundle(advanced))
         upper, grown = orthonormalize(gram, neurons, vectors)
         growth = growth + grown
@@ -487,8 +562,9 @@
             scaled = (state * slope[t + 1][..., None]).astype(jnp.bfloat16)
             edges = [
                 (rotated(edge) * edge_slope[k][t + 1][..., None]).astype(jnp.bfloat16)
-                for k, edge in enumerate(edges)
+                for k, edge in enumerate(beside + over)
             ]
+            beside, over = edges[:2], edges[2:]
             far = (rotated(far) * far_slope[:, t + 1, :, None]).astype(jnp.bfloat16)
     return state[None], growth
 

time: 278 us -> 277 us (level)
  Pallas kernels: 132 us -> 195 us
  waiting for transfers between devices: 46.4 us -> 2.48 us
  starting transfers between devices: 47.7 us -> 37.2 us
  other arithmetic: 12.7 us -> 7.48 us
  local copies, waits for them, and re-layouts: 17.6 us -> 13.9 us
    pallas_call x0 -> x1, Pallas kernels: none -> 64.2 us  [exchanged_together(): pl.pallas_call(functools.partial(exchange_kernel, parts), out_shape=tuple...]
    ppermute x12, waiting for transfers between devices: 25.7 us -> 2.47 us  [shifted(): return lax.ppermute(value, axis, pairs)]
    all_to_all x4 -> x1, waiting for transfers between devices: 20.7 us -> 0.01 us  [exchanged(): return lax.all_to_all(value, 'col', split_axis=0, concat_axis=0, tiled=True)]
    all_to_all x4 -> x1, starting transfers between devices: 21.3 us -> 5.04 us  [exchanged(): return lax.all_to_all(value, 'col', split_axis=0, concat_axis=0, tiled=True)]
    ppermute x12, starting transfers between devices: 26.3 us -> 32.2 us  [shifted(): return lax.ppermute(value, axis, pairs)]
    unnamed x22 -> x47, local copies, waits for them, and re-layouts: 10.4 us -> 8.93 us
  transfers between devices with their start and end apart: 16 -> 13, of which waited for: 5 -> 1; matrix products, arithmetic and copies ran while one was open for 12% -> 9% of each run, Pallas kernels for 9% -> 43%
where the time goes in v4:
time: 277 us; the launch traced here: 276 us
  Pallas kernels  195 us (70%)
  starting transfers between devices  37.2 us (13%)
  matrix products  18.9 us (7%)
  local copies, waits for them, and re-layouts  13.9 us (5%)
  other arithmetic  7.48 us (3%)
    pallas_call x1, Pallas kernels, exchanged_together(): pl.pallas_call(functools.partial(exchange_kernel, parts), out_shape=tuple...  64.2 us
    pallas_call x2, Pallas kernels, summed(): pl.pallas_call(functools.partial(sum_kernel, groups, per_col), out_shape=...  55.6 us
    pallas_call x2, Pallas kernels, orthonormalize(): pl.pallas_call(functools.partial(orthonormal_kernel, count), out_shape=(j...  44 us
    ppermute x12, starting transfers between devices, shifted(): return lax.ppermute(value, axis, pairs)  32.2 us
    pallas_call x2, Pallas kernels, advance(): pl.pallas_call(functools.partial(advance_kernel, per_step), grid=(blocks...  28.8 us
    dot_general x7, matrix products, rotated(): jnp.dot(cells, upper, preferred_element_type=jnp.float32)  16.9 us
    unnamed x47, local copies, waits for them, and re-layouts  8.93 us
  transfers between devices with their start and end apart: 13, of which 1 were waited for; matrix products, arithmetic and copies ran while one was open for 9% of the time, Pallas kernels for 43%

profile of v4, /device:TPU:25, one launch (start us, length us, event | category | flops | bytes accessed | tf_op | source)
XLA Modules:
  0.0 275.9 jit_solution(2856399531494304350)
XLA Ops:
  1.4 3.4 %multiply_convert_fusion.3.own_ref = bf16[16,128,512]{2,1,0:T(8,128)(2,1)} fusion(f32[16,128]{1,0:T(8,128)S(1)} %get-tuple-element.59, bf16[1,16,128,512]{3,2,1,0:T(8,128)(2,1)} %param.9), kind=kLoop, calls=%fused_computation.6 | loop fusion | flops 3145728 | bytes 4202496 | tf_op jit(solution)/shard_map/convert_element_type | solution.py:496
  4.8 3.8 %collective-permute-start.2 = (bf16[16,128,512]{2,1,0:T(8,128)(2,1)}, bf16[16,128,512]{2,1,0:T(8,128)(2,1)}, u32[]{:S(2)}, u32[]{:S(2)}) collective-permute-start(bf16[16,128,512]{2,1,0:T(8,128)(2,1)} %multiply_convert_fusion.3.own_ref), channel_id=1, source_target_pairs={{0,1},{1,2},{2,3},{4,5},{5,6},{6,7},{8,9},{9,10},{10,11},{12,13},{... | collective-permute-start | bytes 6291464 | tf_op jit(solution)/shard_map/ppermute | solution.py:256
  8.6 2.0 collective-permute-start.3
  11.7 1.3 collective-permute-start
  14.9 1.4 copy.33
  17.0 2.4 copy.37
  19.5 1.2 copy.36
  25.2 1.6 maximum_maximum_fusion.1
  26.8 64.2 %exchange.1 = (bf16[8,8,128,128]{3,2,1,0:T(8,128)(2,1)S(1)}, bf16[8,128,512]{2,1,0:T(8,128)(2,1)S(1)}, f32[8,8,128]{2,1,0:T(8,128)S(1)}) custom-call(bf16[8,8,128,128]{3,2,1,0:T(8,128)(2,1)S(1)} %copy.46, bf16[8,128,512]{2,1,0:T(8,128)(2,1)S(1)} %bitcast.110, f32[8,8,128]{2,1,0:T(8,128)S(1)} %pad.9.refs_2_), custom_call_target="tpu_custom_call" | custom-call | bytes 200000000 | tf_op jit(solution)/shard_map/exchange/pallas_call | solution.py:398
  91.1 2.0 place_pairs.1.far_weights_ref
  93.1 2.0 copy-done
  95.1 14.4 %advance.2 = (bf16[16,128,512]{2,1,0:T(8,128)(2,1)S(1)}, f32[1280,128]{1,0:T(8,128)S(1)}) custom-call(bf16[16,128,512]{2,1,0:T(8,128)(2,1)} %bitcast.114, bf16[2,128,512]{2,1,0:T(8,128)(2,1)S(1)} %collective-permute-done.before_ref, bf16[16,128,512]{2,1,0:T(8,128)(2,1)} %multiply_convert_fusion.3.own_ref, ...), custom_call_target="tpu_custom_call" | custom-call | tf_op jit(solution)/shard_map/advance/pallas_call | solution.py:322
  109.6 8.9 %collective-permute-start.4 = (bf16[2,128,512]{2,1,0:T(8,128)(2,1)S(1)}, bf16[2,128,512]{2,1,0:T(8,128)(2,1)S(1)}, u32[]{:S(2)}, u32[]{:S(2)}) collective-permute-start(bf16[2,128,512]{2,1,0:T(8,128)(2,1)S(1)} %get-tuple-element.51), channel_id=1, source_target_pairs={{0,4},{4,8},{8,12},{12,16},{16,20},{20,24},{24,28},{28,0},{1,5},{5... | collective-permute-start | bytes 786440 | tf_op jit(solution)/shard_map/ppermute | solution.py:256
  118.4 4.3 %collective-permute-start.8 = (f32[16,2,128]{2,0,1:T(8,128)S(1)}, f32[16,2,128]{2,0,1:T(8,128)S(1)}, u32[]{:S(2)}, u32[]{:S(2)}) collective-permute-start(f32[16,2,128]{2,0,1:T(8,128)S(1)} %fusion.37), channel_id=1, source_target_pairs={{0,1},{1,2},{2,3},{4,5},{5,6},{6,7},{8,9},{9,10},{10,11},{12,13},{... | collective-permute-start | bytes 49160 | tf_op jit(solution)/shard_map/ppermute | solution.py:256
  122.8 1.9 collective-permute-start.9
  124.7 1.8 collective-permute-start.6
  126.5 2.4 collective-permute-done.6
  128.9 1.5 collective-permute-start.7
  130.5 29.3 %sum_gram.2.packed_ref = f32[1280,128]{1,0:T(8,128)S(1)} custom-call(f32[1280,128]{1,0:T(8,128)S(1)} %get-tuple-element.34.packed_ref), custom_call_target="tpu_custom_call" | custom-call | bytes 80000000 | tf_op jit(solution)/shard_map/sum_gram/pallas_call | solution.py:134
  159.9 2.1 collective-permute-start.11
  162.0 3.5 %collective-permute-start.10 = (bf16[16,128,512]{2,1,0:T(8,128)(2,1)S(1)}, bf16[16,128,512]{2,1,0:T(8,128)(2,1)}, u32[]{:S(2)}, u32[]{:S(2)}) collective-permute-start(bf16[16,128,512]{2,1,0:T(8,128)(2,1)S(1)} %get-tuple-element.36), channel_id=1, source_target_pairs={{0,1},{1,2},{2,3},{4,5},{5,6},{6,7},{8,9},{9,10},{10,11},{12,13},{... | collective-permute-start | bytes 6291464 | tf_op jit(solution)/shard_map/ppermute | solution.py:256
  167.2 1.3 copy.32
  168.5 5.0 %all-to-all-start = ((bf16[8,128,512]{2,1,0:T(8,128)(2,1)}), bf16[8,128,512]{2,1,0:T(8,128)(2,1)}, u32[]{:S(2)}, u32[]{:S(2)}) async-start(bf16[8,128,512]{2,1,0:T(8,128)(2,1)} %copy.32), calls=%async_computation | async-start | bytes 2097152 | tf_op jit(solution)/shard_map/all_to_all | solution.py:268
  173.6 21.9 %orthonormalize.2 = (bf16[512,512]{1,0:T(8,128)(2,1)S(1)}, f32[1,512]{1,0:T(1,128)S(1)}) custom-call(f32[1280,128]{1,0:T(8,128)S(1)} %sum_gram.2.packed_ref), custom_call_target="tpu_custom_call" | custom-call | flops 30000001024 | bytes 90000000 | tf_op jit(solution)/shard_map/orthonormalize/pallas_call | solution.py:228
  196.2 3.3 %multiply_convert_fusion.2 = (bf16[16,128,512]{2,1,0:T(8,128)(2,1)}, bf16[16,128,512]{2,1,0:T(8,128)(2,1)}) fusion(f32[16,128]{1,0:T(8,128)S(1)} %get-tuple-element.58, bf16[16,128,512]{2,1,0:T(8,128)(2,1)S(1)} %get-tuple-element.36, bf16[512,512]{1,0:T(8,128)(2,1)S(1)} %get-tuple-element.38), kind=kOutput, calls=%fused_computation.5 | convolution fusion | flops 1077936128 | bytes 6823936 | tf_op jit(solution)/shard_map/dot_general | solution.py:558
  199.4 1.9 multiply_convert_fusion.6
  201.4 4.2 %multiply_convert_fusion.below_ref = bf16[16,128,512]{2,1,0:T(8,128)(2,1)} fusion(f32[16,128]{1,0:T(8,128)S(1)} %get-tuple-element.77, bf16[16,128,512]{2,1,0:T(8,128)(2,1)} %collective-permute-done.11, bf16[512,512]{1,0:T(8,128)(2,1)S(1)} %get-tuple-element.38), kind=kOutput, calls=%fused_computation.3 | convolution fusion | flops 1077936128 | bytes 4726784 | tf_op jit(solution)/shard_map/dot_general | solution.py:558
  205.6 4.3 %multiply_convert_fusion.1.above_ref = bf16[16,128,512]{2,1,0:T(8,128)(2,1)} fusion(f32[16,128]{1,0:T(8,128)S(1)} %get-tuple-element.78, bf16[16,128,512]{2,1,0:T(8,128)(2,1)} %collective-permute-done.10, bf16[512,512]{1,0:T(8,128)(2,1)S(1)} %get-tuple-element.38), kind=kOutput, calls=%fused_computation.4 | convolution fusion | flops 1077936128 | bytes 4726784 | tf_op jit(solution)/shard_map/dot_general | solution.py:558
  210.0 14.4 %advance.3 = (bf16[16,128,512]{2,1,0:T(8,128)(2,1)S(1)}, f32[1280,128]{1,0:T(8,128)S(1)}) custom-call(bf16[16,128,512]{2,1,0:T(8,128)(2,1)} %get-tuple-element.76.tangents_ref, bf16[2,128,512]{2,1,0:T(8,128)(2,1)S(1)} %fusion.6.before_ref, bf16[16,128,512]{2,1,0:T(8,128)(2,1)} %get-tuple-element.75.own_ref, bf16[2,128,512]{2,1,0:T(8,128)(2,1)S(1)} %fusion.3.after_ref, ...), custom_call_target="tpu_custom_call" | custom-call | tf_op jit(solution)/shard_map/advance/pallas_call | solution.py:322
  224.4 26.3 %sum_gram.3.packed_ref = f32[1280,128]{1,0:T(8,128)S(1)} custom-call(f32[1280,128]{1,0:T(8,128)S(1)} %get-tuple-element.46.packed_ref), custom_call_target="tpu_custom_call" | custom-call | bytes 80000000 | tf_op jit(solution)/shard_map/sum_gram/pallas_call | solution.py:134
  250.6 22.1 %orthonormalize.3 = (bf16[512,512]{1,0:T(8,128)(2,1)S(1)}, f32[1,512]{1,0:T(1,128)S(1)}) custom-call(f32[1280,128]{1,0:T(8,128)S(1)} %sum_gram.3.packed_ref), custom_call_target="tpu_custom_call" | custom-call | flops 30000001024 | bytes 90000000 | tf_op jit(solution)/shard_map/orthonormalize/pallas_call | solution.py:228
  273.3 2.6 convert_bitcast_fusion
  (99 shorter events, 11.9 us)
Async XLA Ops:
  1.4 12.7 %copy-start.13 = (s32[4,128]{1,0:T(4,128)S(1)}, s32[4,128]{1,0:T(4,128)}, u32[]{:S(2)}) copy-start(s32[4,128]{1,0:T(4,128)} %param.13) | copy-start | bytes 6148
  1.4 13.1 %copy-start.8 = (f32[2,1,16,128]{3,2,1,0:T(8,128)S(1)}, f32[2,1,16,128]{3,2,1,0:T(8,128)}, u32[]{:S(2)}) copy-start(f32[2,1,16,128]{3,2,1,0:T(8,128)} %param.11) | copy-start | bytes 49156
  4.8 11.5 %copy-start.19 = (s32[1,1,32,1]{2,3,1,0:T(1,128)S(1)}, s32[1,1,32,1]{2,3,1,0:T(1,128)}, u32[]{:S(2)}) copy-start(s32[1,1,32,1]{2,3,1,0:T(1,128)} %param.14) | copy-start | bytes 388
  4.8 11.7 %copy-start.20 = (s32[1,1,32]{2,1,0:T(1,128)S(1)}, s32[1,1,32]{2,1,0:T(1,128)}, u32[]{:S(2)}) copy-start(s32[1,1,32]{2,1,0:T(1,128)} %param.15) | copy-start | bytes 388
  4.8 90.3 %collective-permute-start.2 = (bf16[16,128,512]{2,1,0:T(8,128)(2,1)}, bf16[16,128,512]{2,1,0:T(8,128)(2,1)}, u32[]{:S(2)}, u32[]{:S(2)}) collective-permute-start(bf16[16,128,512]{2,1,0:T(8,128)(2,1)} %multiply_convert_fusion.3.own_ref), channel_id=1, source_target_pairs={{0,1},{1,2},{2,3},{4,5},{5,6},{6,7},{8,9},{9,10},{10,11},{12,13},{... | collective-permute-start | bytes 6291464 | tf_op jit(solution)/shard_map/ppermute | solution.py:256
  8.6 86.5 %collective-permute-start.3 = (bf16[16,128,512]{2,1,0:T(8,128)(2,1)}, bf16[16,128,512]{2,1,0:T(8,128)(2,1)}, u32[]{:S(2)}, u32[]{:S(2)}) collective-permute-start(bf16[16,128,512]{2,1,0:T(8,128)(2,1)} %multiply_convert_fusion.3.own_ref), channel_id=1, source_target_pairs={{1,0},{2,1},{3,2},{5,4},{6,5},{7,6},{9,8},{10,9},{11,10},{13,12},{... | collective-permute-start | bytes 6291464 | tf_op jit(solution)/shard_map/ppermute | solution.py:256
  11.7 15.1 %collective-permute-start = (bf16[2,128,512]{2,1,0:T(8,128)(2,1)S(1)}, bf16[2,128,512]{2,1,0:T(8,128)(2,1)S(1)}, u32[]{:S(2)}, u32[]{:S(2)}) collective-permute-start(bf16[2,128,512]{2,1,0:T(8,128)(2,1)S(1)} %get-tuple-element.53), channel_id=1, source_target_pairs={{0,4},{4,8},{8,12},{12,16},{16,20},{20,24},{24,28},{28,0},{1,5},{5... | collective-permute-start | bytes 786440 | tf_op jit(solution)/shard_map/ppermute | solution.py:256
  13.0 13.8 %collective-permute-start.1 = (bf16[2,128,512]{2,1,0:T(8,128)(2,1)S(1)}, bf16[2,128,512]{2,1,0:T(8,128)(2,1)S(1)}, u32[]{:S(2)}, u32[]{:S(2)}) collective-permute-start(bf16[2,128,512]{2,1,0:T(8,128)(2,1)S(1)} %get-tuple-element.52), channel_id=1, source_target_pairs={{0,28},{4,0},{8,4},{12,8},{16,12},{20,16},{24,20},{28,24},{1,29},{... | collective-permute-start | bytes 786440 | tf_op jit(solution)/shard_map/ppermute | solution.py:256
  17.0 2.5 copy-start.2
  19.4 1.2 copy-start.14
  24.0 1.2 copy-start.3
  93.1 2.0 copy-start
  109.6 50.3 %collective-permute-start.4 = (bf16[2,128,512]{2,1,0:T(8,128)(2,1)S(1)}, bf16[2,128,512]{2,1,0:T(8,128)(2,1)S(1)}, u32[]{:S(2)}, u32[]{:S(2)}) collective-permute-start(bf16[2,128,512]{2,1,0:T(8,128)(2,1)S(1)} %get-tuple-element.51), channel_id=1, source_target_pairs={{0,4},{4,8},{8,12},{12,16},{16,20},{20,24},{24,28},{28,0},{1,5},{5... | collective-permute-start | bytes 786440 | tf_op jit(solution)/shard_map/ppermute | solution.py:256
  118.4 41.5 %collective-permute-start.5 = (bf16[2,128,512]{2,1,0:T(8,128)(2,1)S(1)}, bf16[2,128,512]{2,1,0:T(8,128)(2,1)S(1)}, u32[]{:S(2)}, u32[]{:S(2)}) collective-permute-start(bf16[2,128,512]{2,1,0:T(8,128)(2,1)S(1)} %get-tuple-element.50), channel_id=1, source_target_pairs={{0,28},{4,0},{8,4},{12,8},{16,12},{20,16},{24,20},{28,24},{1,29},{... | collective-permute-start | bytes 786440 | tf_op jit(solution)/shard_map/ppermute | solution.py:256
  118.4 41.4 %collective-permute-start.8 = (f32[16,2,128]{2,0,1:T(8,128)S(1)}, f32[16,2,128]{2,0,1:T(8,128)S(1)}, u32[]{:S(2)}, u32[]{:S(2)}) collective-permute-start(f32[16,2,128]{2,0,1:T(8,128)S(1)} %fusion.37), channel_id=1, source_target_pairs={{0,1},{1,2},{2,3},{4,5},{5,6},{6,7},{8,9},{9,10},{10,11},{12,13},{... | collective-permute-start | bytes 49160 | tf_op jit(solution)/shard_map/ppermute | solution.py:256
  122.8 37.1 %collective-permute-start.9 = (f32[16,2,128]{2,0,1:T(8,128)S(1)}, f32[16,2,128]{2,0,1:T(8,128)S(1)}, u32[]{:S(2)}, u32[]{:S(2)}) collective-permute-start(f32[16,2,128]{2,0,1:T(8,128)S(1)} %fusion.37), channel_id=1, source_target_pairs={{1,0},{2,1},{3,2},{5,4},{6,5},{7,6},{9,8},{10,9},{11,10},{13,12},{... | collective-permute-start | bytes 49160 | tf_op jit(solution)/shard_map/ppermute | solution.py:256
  124.7 4.2 %collective-permute-start.6 = (f32[2,2,128]{2,0,1:T(2,128)S(1)}, f32[2,2,128]{2,0,1:T(2,128)S(1)}, u32[]{:S(2)}, u32[]{:S(2)}) collective-permute-start(f32[2,2,128]{2,0,1:T(2,128)S(1)} %get-tuple-element.61), channel_id=1, source_target_pairs={{0,4},{4,8},{8,12},{12,16},{16,20},{20,24},{24,28},{28,0},{1,5},{5... | collective-permute-start | bytes 6152 | tf_op jit(solution)/shard_map/ppermute | solution.py:256
  128.9 37.7 %copy-start.15 = (f32[2,2,128]{2,0,1:T(2,128)}, f32[2,2,128]{2,0,1:T(2,128)S(1)}, u32[]{:S(2)}) copy-start(f32[2,2,128]{2,0,1:T(2,128)S(1)} %collective-permute-done.6) | copy-start | bytes 6148
  128.9 30.9 %collective-permute-start.7 = (f32[2,2,128]{2,0,1:T(2,128)S(1)}, f32[2,2,128]{2,0,1:T(2,128)S(1)}, u32[]{:S(2)}, u32[]{:S(2)}) collective-permute-start(f32[2,2,128]{2,0,1:T(2,128)S(1)} %get-tuple-element.60), channel_id=1, source_target_pairs={{0,28},{4,0},{8,4},{12,8},{16,12},{20,16},{24,20},{28,24},{1,29},{... | collective-permute-start | bytes 6152 | tf_op jit(solution)/shard_map/ppermute | solution.py:256
  159.8 6.8 %copy-start.17 = (f32[2,2,128]{2,0,1:T(2,128)}, f32[2,2,128]{2,0,1:T(2,128)S(1)}, u32[]{:S(2)}) copy-start(f32[2,2,128]{2,0,1:T(2,128)S(1)} %collective-permute-done.7) | copy-start | bytes 6148
  159.8 6.8 %copy-start.9 = (f32[16,2,128]{2,0,1:T(8,128)}, f32[16,2,128]{2,0,1:T(8,128)S(1)}, u32[]{:S(2)}) copy-start(f32[16,2,128]{2,0,1:T(8,128)S(1)} %collective-permute-done.8) | copy-start | bytes 49156
  159.9 6.8 %copy-start.11 = (f32[16,2,128]{2,0,1:T(8,128)}, f32[16,2,128]{2,0,1:T(8,128)S(1)}, u32[]{:S(2)}) copy-start(f32[16,2,128]{2,0,1:T(8,128)S(1)} %collective-permute-done.9) | copy-start | bytes 49156
  159.9 6.8 %copy-start.5 = (bf16[2,128,512]{2,1,0:T(8,128)(2,1)}, bf16[2,128,512]{2,1,0:T(8,128)(2,1)S(1)}, u32[]{:S(2)}) copy-start(bf16[2,128,512]{2,1,0:T(8,128)(2,1)S(1)} %collective-permute-done.5) | copy-start | bytes 786436
  159.9 41.5 %collective-permute-start.11 = (bf16[16,128,512]{2,1,0:T(8,128)(2,1)S(1)}, bf16[16,128,512]{2,1,0:T(8,128)(2,1)}, u32[]{:S(2)}, u32[]{:S(2)}) collective-permute-start(bf16[16,128,512]{2,1,0:T(8,128)(2,1)S(1)} %get-tuple-element.36), channel_id=1, source_target_pairs={{1,0},{2,1},{3,2},{5,4},{6,5},{7,6},{9,8},{10,9},{11,10},{13,12},{... | collective-permute-start | bytes 6291464 | tf_op jit(solution)/shard_map/ppermute | solution.py:256
  162.0 43.6 %collective-permute-start.10 = (bf16[16,128,512]{2,1,0:T(8,128)(2,1)S(1)}, bf16[16,128,512]{2,1,0:T(8,128)(2,1)}, u32[]{:S(2)}, u32[]{:S(2)}) collective-permute-start(bf16[16,128,512]{2,1,0:T(8,128)(2,1)S(1)} %get-tuple-element.36), channel_id=1, source_target_pairs={{0,1},{1,2},{2,3},{4,5},{5,6},{6,7},{8,9},{9,10},{10,11},{12,13},{... | collective-permute-start | bytes 6291464 | tf_op jit(solution)/shard_map/ppermute | solution.py:256
  168.5 30.9 %all-to-all-start = ((bf16[8,128,512]{2,1,0:T(8,128)(2,1)}), bf16[8,128,512]{2,1,0:T(8,128)(2,1)}, u32[]{:S(2)}, u32[]{:S(2)}) async-start(bf16[8,128,512]{2,1,0:T(8,128)(2,1)} %copy.32), calls=%async_computation | async-start | bytes 2097152 | tf_op jit(solution)/shard_map/all_to_all | solution.py:268
  173.6 21.9 %copy-start.16 = (f32[2,2,128]{2,0,1:T(2,128)S(1)}, f32[2,2,128]{2,0,1:T(2,128)}, u32[]{:S(2)}) copy-start(f32[2,2,128]{2,0,1:T(2,128)} %copy-done.15) | copy-start | bytes 6148
  173.6 21.9 %copy-start.18 = (f32[2,2,128]{2,0,1:T(2,128)S(1)}, f32[2,2,128]{2,0,1:T(2,128)}, u32[]{:S(2)}) copy-start(f32[2,2,128]{2,0,1:T(2,128)} %copy-done.17) | copy-start | bytes 6148
  173.6 22.0 %copy-start.10 = (f32[16,2,128]{2,0,1:T(8,128)S(1)}, f32[16,2,128]{2,0,1:T(8,128)}, u32[]{:S(2)}) copy-start(f32[16,2,128]{2,0,1:T(8,128)} %copy-done.9) | copy-start | bytes 49156
  173.6 22.0 %copy-start.12 = (f32[16,2,128]{2,0,1:T(8,128)S(1)}, f32[16,2,128]{2,0,1:T(8,128)}, u32[]{:S(2)}) copy-start(f32[16,2,128]{2,0,1:T(8,128)} %copy-done.11) | copy-start | bytes 49156
  173.6 22.0 %copy-start.6 = (bf16[2,128,512]{2,1,0:T(8,128)(2,1)S(1)}, bf16[2,128,512]{2,1,0:T(8,128)(2,1)}, u32[]{:S(2)}) copy-start(bf16[2,128,512]{2,1,0:T(8,128)(2,1)} %copy-done.5) | copy-start | bytes 786436
  205.6 4.3 %copy-start.1 = (f32[16,128,16]{2,1,0:T(8,128)S(1)}, f32[16,128,16]{2,1,0:T(8,128)}, u32[]{:S(2)}) copy-start(f32[16,128,16]{2,1,0:T(8,128)} %get-tuple-element.73.coef_ref) | copy-start | bytes 393220
  (2 other events, 1.9 us)
